TPU v7x, 256 devices: a whole 4x4x8 slice. The times are simulated.
256 devices in a mesh: row: 8 (over z_hi, core), col: 32 (over z_lo, x, y).
Axes of the slice: x: 4, y: 4, z: 8 (z_hi: 4, z_lo: 2; z = z_hi * 2 + z_lo), core: 2. Of those that a mesh axis runs over, the one named last changes fastest.
Arguments:
- features: float32 [32, 1024, 128], P('col', 'row'), may hold values from -6 to 6
- block_values: float32 [8, 32, 160, 128, 128], P('row', 'col'), may hold values from -0.0390625 to 0.0390625
- block_rows: int32 [8, 32, 160], P('row', 'col'), may hold values from 0 to 31
- block_cols: int32 [8, 32, 160], P('row', 'col'), may hold values from 0 to 7
- live_block_count: int32 [8, 32], P('row', 'col'), may hold values from 1 to 160, as said below
- weight: float32 [128, 128], replicated, may hold values from -0.5 to 0.5
- cotangent: float32 [8, 4096, 128], P('row', 'col'), may hold values from -6 to 6
Outputs:
- activated: float32 [8, 4096, 128], P('row', 'col')
- weight_grad: float32 [128, 128], replicated
- feature_grad: float32 [32, 1024, 128], P('col', 'row')
Inputs may be any that keep to these rules, and one draw needn't show every extreme that they name: `live_block_count`: some tile has all 160 slots live.
All inputs are finite; a program needn't handle non-finite values.
Results may differ from a plain program's by a relative error of at most 0.0003.
Values sent between devices are 32-bit elements; how exact they have to be, the bound alone decides.
A program may use at most 128 MiB of HBM per device.

v0:
```python
import jax
import jax.numpy as jnp
from jax import lax
from jax.sharding import PartitionSpec as P


def silu_grad(z_vals):
    sig = jax.nn.sigmoid(z_vals)
    return sig * (1.0 + z_vals * (1.0 - sig))


def local(features, block_values, block_rows, block_cols, live_block_count, weight, cotangent):
    hp = lax.Precision.HIGHEST
    own_feats = features[0]
    entry_values = block_values[0, 0]
    brows = block_rows[0, 0]
    bcols = block_cols[0, 0]
    slot_capacity = entry_values.shape[0]
    bsize = entry_values.shape[1]
    width = own_feats.shape[1]
    is_live_slot = jnp.arange(slot_capacity, dtype=jnp.int32) < live_block_count[0, 0]
    gathered = lax.all_gather(own_feats, "row", axis=0, tiled=True)
    col_blocks = gathered.reshape(-1, bsize, width)
    chosen = jnp.take(col_blocks, bcols, axis=0)
    forward_prods = jnp.einsum("kij,kjf->kif", entry_values, chosen, precision=hp)
    own_rows = own_feats.shape[0]
    nblk = lax.axis_size("col") * own_rows // bsize
    ids = jnp.arange(nblk, dtype=jnp.int32)
    onehot = ((brows[None, :] == ids[:, None]) & is_live_slot[None, :]).astype(jnp.float32)
    reduced = lax.psum_scatter(
        jnp.einsum("bk,kif->bif", onehot, forward_prods, precision=hp).reshape(
            lax.axis_size("col") * own_rows, width
        ),
        "col",
        scatter_dimension=0,
        tiled=True,
    )
    z_vals = jnp.dot(reduced, weight, precision=hp, preferred_element_type=jnp.float32)
    activated = jax.nn.silu(z_vals)
    dz_vals = cotangent[0] * silu_grad(z_vals)
    back_source = jnp.dot(dz_vals, weight.T, precision=hp, preferred_element_type=jnp.float32)
    tile_grads = lax.all_gather(back_source, "col", axis=0, tiled=True)
    row_blocks = tile_grads.reshape(-1, bsize, width)
    picked = jnp.take(row_blocks, brows, axis=0)
    backward_prods = jnp.einsum("kji,kjf->kif", entry_values, picked, precision=hp)
    nblk = lax.axis_size("row") * own_rows // bsize
    ids = jnp.arange(nblk, dtype=jnp.int32)
    onehot = ((bcols[None, :] == ids[:, None]) & is_live_slot[None, :]).astype(jnp.float32)
    summed_back = lax.psum_scatter(
        jnp.einsum("bk,kif->bif", onehot, backward_prods, precision=hp).reshape(
            lax.axis_size("row") * own_rows, width
        ),
        "row",
        scatter_dimension=0,
        tiled=True,
    )
    weight_term = jnp.dot(reduced.T, dz_vals, precision=hp, preferred_element_type=jnp.float32)
    weight_grad = lax.psum(weight_term, ("row", "col"))
    return (activated[None], weight_grad, summed_back[None])


def solution(mesh):
    in_specs = (
        P("col", "row", None),
        P("row", "col", None, None, None),
        P("row", "col", None),
        P("row", "col", None),
        P("row", "col"),
        P(),
        P("row", "col", None),
    )
    out_specs = (P("row", "col", None), P(), P("col", "row", None))
    return jax.shard_map(local, mesh=mesh, in_specs=in_specs, out_specs=out_specs, check_vma=False)
```

profile of v0, /device:TPU:1, one launch (start us, length us, event | category | flops | bytes accessed | tf_op | source)
XLA Modules:
  0.0 689.0 jit_solution(4359490509392069261)
XLA Ops:
  7.2 0.0 copy-start
  7.2 0.0 reduce-scatter.3.cloned.1.call-start
  7.9 0.7 compare_select_fusion.1
  8.6 0.7 compare_and_fusion.1
  9.3 20.2 %all-gather = f32[1,1024,128]{2,1,0:T(8,128)S(1)} all-gather(f32[1,128,128]{2,1,0:T(8,128)} %param.7), channel_id=2, replica_groups=mesh['row'=8,'col'=32] {'row'}, dimensions={1}, use_global_device_ids=true | all-gather | bytes 589824 | tf_op jit(solution)/shard_map/all_gather | solution.py:22
  29.4 5.1 gather_fusion
  34.5 26.2 %fusion.6 = f32[160,128,128]{2,1,0:T(8,128)} fusion(f32[1,1,160,128,128]{4,3,2,1,0:T(8,128)} %param.8, f32[160,128,128]{2,1,0:T(8,128)} %gather_fusion, pred[160]{0:T(512)(128)(4,1)S(1)} %compare_and_fusion.1), kind=kOutput, calls=%fused_computation.8 | convolution fusion | flops 4029153280 | bytes 31457440 | tf_op jit(solution)/shard_map/kij,kjf->kif/dot_general | solution.py:25
  60.7 0.0 copy-start.2
  60.7 11.5 %copy.12 = f32[160,128,128]{1,0,2:T(8,128)} copy(f32[160,128,128]{2,1,0:T(8,128)} %fusion.6) | data formatting | bytes 20971520 | tf_op jit(solution)/shard_map/kij,kjf->kif/dot_general | solution.py:25
  72.2 0.0 copy-start.4
  72.2 0.0 copy-done.2
  72.2 6.7 fusion.2
  79.0 2.6 copy.10
  81.5 0.0 reduce-scatter.3.cloned.1.call-update
  81.5 0.0 all-gather.3.cloned.1.call-start
  81.6 140.7 %reduce-scatter.3.cloned.1.call-done = f32[128,128]{1,0:T(8,128)} async-done(((f32[4096,128]{1,0:T(8,128)}), f32[128,128]{1,0:T(8,128)}) %reduce-scatter.3.cloned.1.call-update) | async-done | bytes 65552 | tf_op jit(solution)/shard_map/reduce_scatter | solution.py:30
  222.2 0.0 copy-done
  222.2 1.0 fusion.28
  223.3 0.0 copy-done.4
  223.3 0.9 fusion.26
  224.2 0.0 all-gather.3.cloned.1.call-update
  224.2 0.0 all-reduce.2.cloned.1.call-start
  224.3 1.8 fusion.27
  226.1 0.0 all-reduce.2.cloned.1.call-update
  226.1 0.0 reduce-scatter.5.cloned.1.call-start
  226.1 154.1 %all-gather.3.cloned.1.call-done = f32[4096,128]{1,0:T(8,128)} async-done(((f32[128,128]{1,0:T(8,128)}), f32[4096,128]{1,0:T(8,128)}) %all-gather.3.cloned.1.call-update) | async-done | bytes 2097168 | tf_op jit(solution)/shard_map/all_gather | solution.py:42
  380.3 11.7 %gather_fusion.1 = f32[160,128,128]{2,1,0:T(8,128)} fusion(f32[32,128,128]{2,1,0:T(8,128)} %bitcast.43, s32[1024]{0:T(1024)S(1)} %pad_clamp_fusion), kind=kCustom, calls=%fused_computation.1 | custom fusion | bytes 20972160 | tf_op jit(solution)/shard_map/jit(_take)/gather | solution.py:44
  392.0 23.8 %fusion.4 = f32[160,128,128]{2,1,0:T(8,128)} fusion(f32[1,1,160,128,128]{4,3,2,1,0:T(8,128)} %param.8, f32[160,128,128]{2,1,0:T(8,128)} %gather_fusion.1, pred[160]{0:T(512)(128)(4,1)S(1)} %compare_and_fusion), kind=kOutput, calls=%fused_computation.6 | convolution fusion | flops 4029153280 | bytes 31457440 | tf_op jit(solution)/shard_map/kji,kjf->kif/dot_general | solution.py:45
  415.8 0.0 copy-start.3
  415.8 0.0 copy-start.1
  415.8 11.5 %copy.13 = f32[160,128,128]{1,0,2:T(8,128)} copy(f32[160,128,128]{2,1,0:T(8,128)} %fusion.4) | data formatting | bytes 20971520 | tf_op jit(solution)/shard_map/kji,kjf->kif/dot_general | solution.py:45
  427.3 0.0 copy-done.3
  427.3 6.1 fusion
  433.4 0.9 copy.11
  434.3 0.0 reduce-scatter.5.cloned.1.call-update
  434.3 0.7 multiply_bitcast_fusion
  435.0 211.0 %all-reduce.2.cloned.1.call-done = f32[128,128]{1,0:T(8,128)} async-done(((f32[128,128]{1,0:T(8,128)}), f32[128,128]{1,0:T(8,128)}) %all-reduce.2.cloned.1.call-update) | async-done | bytes 65552 | tf_op jit(solution)/shard_map/psum | solution.py:58
  646.0 35.0 %reduce-scatter.5.cloned.1.call-done = f32[128,128]{1,0:T(8,128)} async-done(((f32[1024,128]{1,0:T(8,128)}), f32[128,128]{1,0:T(8,128)}) %reduce-scatter.5.cloned.1.call-update) | async-done | bytes 65552 | tf_op jit(solution)/shard_map/reduce_scatter | solution.py:49
  681.0 1.5 copy.16
  682.5 0.0 copy-done.1
  (5 shorter events, 0.0 us)
Async XLA Ops:
  7.2 215.1 %copy-start = (f32[128,128]{1,0:T(8,128)S(1)}, f32[128,128]{1,0:T(8,128)}, u32[]{:S(2)}) copy-start(f32[128,128]{1,0:T(8,128)} %param.12) | copy-start | bytes 196612
  7.2 215.1 %reduce-scatter.3.cloned.1.call-start = ((), (), s32[]{:S(2)}) async-start(), calls=%async_computation.2 | async-start | bytes 2162688 | tf_op jit(solution)/shard_map/reduce_scatter | solution.py:30
  60.7 11.5 %copy-start.2 = (s32[1,1,160]{2,1,0:T(1,128)S(1)}, s32[1,1,160]{2,1,0:T(1,128)}, u32[]{:S(2)}) copy-start(s32[1,1,160]{2,1,0:T(1,128)} %param.9) | copy-start | bytes 1924
  72.2 151.1 %copy-start.4 = (f32[1,128,128]{2,1,0:T(8,128)S(1)}, f32[1,128,128]{2,1,0:T(8,128)}, u32[]{:S(2)}) copy-start(f32[1,128,128]{2,1,0:T(8,128)} %param.13) | copy-start | bytes 196612
  81.5 298.7 %all-gather.3.cloned.1.call-start = ((), (), s32[]{:S(2)}) async-start(), calls=%async_computation.4 | async-start | bytes 2162688 | tf_op jit(solution)/shard_map/all_gather | solution.py:42
  224.2 421.7 %all-reduce.2.cloned.1.call-start = ((), (), s32[]{:S(2)}) async-start(), calls=%async_computation.3 | async-start | bytes 131072 | tf_op jit(solution)/shard_map/psum | solution.py:58
  226.1 454.9 %reduce-scatter.5.cloned.1.call-start = ((), (), s32[]{:S(2)}) async-start(), calls=%async_computation.5 | async-start | bytes 589824 | tf_op jit(solution)/shard_map/reduce_scatter | solution.py:49
  415.8 11.5 %copy-start.3 = (s32[1,1,160]{2,1,0:T(1,128)S(1)}, s32[1,1,160]{2,1,0:T(1,128)}, u32[]{:S(2)}) copy-start(s32[1,1,160]{2,1,0:T(1,128)} %param.10) | copy-start | bytes 1924
  415.8 266.7 %copy-start.1 = (f32[128,128]{1,0:T(8,128)S(1)}, f32[128,128]{1,0:T(8,128)}, u32[]{:S(2)}) copy-start(f32[128,128]{1,0:T(8,128)} %param.12) | copy-start | bytes 196612
Sparse Core Ops, SparseCore 0:
  81.7 140.5 reduce-scatter.2
  224.7 155.4 all-gather.2
  387.2 258.6 all-reduce.1
  649.1 31.8 reduce-scatter.4
where the time goes:
time: 691 us; the launch traced here: 689 us
  waiting for transfers between devices  541 us (78%)
  matrix products  66.5 us (10%)
  local copies, waits for them, and re-layouts  44.8 us (6%)
  blocking collectives  20.2 us (3%)
  between operations  14.5 us (2%)
    psum x1, waiting for transfers between devices, local(): weight_grad = lax.psum(weight_term, ('row', 'col'))  211 us
    all_gather x1, waiting for transfers between devices, local(): tile_grads = lax.all_gather(back_source, 'col', axis=0, tiled=True)  154 us
    reduce_scatter x1, waiting for transfers between devices, local(): lax.psum_scatter(jnp.einsum('bk,kif->bif', onehot, forward_prods, precisi...  141 us
    reduce_scatter x1, waiting for transfers between devices, local(): lax.psum_scatter(jnp.einsum('bk,kif->bif', onehot, backward_prods, precis...  35 us
    dot_general x1, matrix products, local(): jnp.einsum('kij,kjf->kif', entry_values, chosen, precision=hp)  26.2 us
    dot_general x1, matrix products, local(): jnp.einsum('kji,kjf->kif', entry_values, picked, precision=hp)  23.8 us
    all_gather x1, blocking collectives, local(): gathered = lax.all_gather(own_feats, 'row', axis=0, tiled=True)  20.2 us
  transfers between devices with their start and end apart: 4, of which 4 were waited for; matrix products, arithmetic and copies ran while one was open for 8% of the time, Pallas kernels for 0%

commit v1 on v0

v1 whole, which is shorter than its diff:
```python
import functools

import jax
import jax.numpy as jnp
from jax import lax
from jax.experimental import pallas as pl
from jax.experimental.pallas import tpu as pltpu
from jax.sharding import PartitionSpec as P

B = 128
SLOTS = 160
COLS = 8
PEERS = 32
ROWS = 8
XY = 16
CHUNK = 20
CHUNKS = SLOTS // CHUNK
F32 = jnp.float32
BF16 = jnp.bfloat16
HP = lax.Precision.HIGHEST


def split(v):
    hi = v.astype(BF16)
    return hi, (v - hi.astype(F32)).astype(BF16)


def kernel(
    prev, idx, feat, weight, cot, values,
    act_out, wgrad_out, fgrad_out,
    land, summed, pieces, xbuf, xx, ysend, yrecv, ysum, pown, precv, facc, srecv, zsend, zrecv,
    wterm, w1, w2, w3,
    asem, xs, xr, ys, yr, ps, pr, ss, sr, zs, zr, w1s, w1r, w2s, w2r, w3s, w3r,
):
    r = lax.axis_index("row")
    c = lax.axis_index("col")
    zh, core = lax.div(r, 2), lax.rem(r, 2)
    zl, x, y = lax.div(c, 16), lax.rem(lax.div(c, 4), 4), lax.rem(c, 4)
    xy = lax.rem(c, XY)
    sib = zh * 2 + (1 - core)

    def col_at(d):
        return (
            lax.rem(zl + lax.div(d, 16), 2) * 16
            + lax.rem(x + lax.rem(lax.div(d, 4), 4), 4) * 4
            + lax.rem(y + lax.rem(d, 4), 4)
        )

    def col_from(d):
        return (
            lax.rem(zl + lax.div(d, 16), 2) * 16
            + lax.rem(x + 4 - lax.rem(lax.div(d, 4), 4), 4) * 4
            + lax.rem(y + 4 - lax.rem(d, 4), 4)
        )

    def to(src, dst, send, recv, row, col):
        return pltpu.make_async_remote_copy(
            src_ref=src, dst_ref=dst, send_sem=send, recv_sem=recv,
            device_id={"row": row, "col": col}, device_id_type=pl.DeviceIdType.MESH,
        )

    def loads(i):
        part = pl.ds(i * CHUNK, CHUNK)
        return pltpu.make_async_copy(values.at[part], land.at[part], asem.at[i])

    for i in range(CHUNKS):
        loads(i).start()

    barrier = pltpu.get_barrier_semaphore()

    @pl.loop(1, PEERS)
    def _(d):
        pl.semaphore_signal(barrier, 1, device_id={"row": r, "col": col_at(d)}, device_id_type=pl.DeviceIdType.MESH)

    @pl.loop(1, ROWS)
    def _(e):
        pl.semaphore_signal(barrier, 1, device_id={"row": lax.rem(r + e, ROWS), "col": c}, device_id_type=pl.DeviceIdType.MESH)

    pl.semaphore_wait(barrier, PEERS - 1 + ROWS - 1)

    def xcopy(src, slot, send, row):
        return to(src, xbuf.at[slot], xs.at[send], xr.at[slot], row, c)

    for dz in range(1, 4):
        xcopy(feat, r, dz, lax.rem(zh + dz, 4) * 2 + core).start()
    xcopy(feat, r, 0, sib).start()
    xbuf[r] = feat[...]

    summed[SLOTS] = jnp.zeros((B, B), F32)
    pieces[SLOTS] = jnp.zeros((B, 2 * B), BF16)

    def prepare(i):
        loads(i).wait()

        @pl.loop(i * CHUNK, (i + 1) * CHUNK)
        def _(k):
            v = land[k] + summed[prev[k]]
            summed[k] = v
            hi, lo = split(v)
            pieces[k, :, :B] = hi
            pieces[k, :, B:] = lo

    for i in range(CHUNKS // 2):
        prepare(i)

    for dz in range(1, 4):
        slot = lax.rem(zh + 4 - dz, 4) * 2 + core
        xcopy(feat, slot, dz, sib).wait_recv()
        xcopy(xbuf.at[slot], slot, 3 + dz, sib).start()

    for i in range(CHUNKS // 2, CHUNKS):
        prepare(i)

    for dz in range(4):
        slot = lax.rem(zh + dz, 4) * 2 + (1 - core)
        xcopy(feat, slot, 0, sib).wait_recv()
    for i in range(COLS):
        hi, lo = split(xbuf[i])
        xx[i, :B, :B] = hi
        xx[i, B:, :B] = hi
        xx[i, :B, B:] = lo
        xx[i, B:, B:] = lo

    def y_block(at):
        acc = jnp.zeros((B, 2 * B), F32)
        for i in range(COLS):
            acc = acc + jnp.dot(pieces[idx[at * COLS + i]], xx[i], preferred_element_type=F32)
        return acc[:, :B] + acc[:, B:]

    def ycopy(d):
        return to(ysend.at[d], yrecv.at[d], ys.at[d], yr.at[d], r, col_at(d))

    @pl.loop(1, PEERS)
    def _(d):
        ysend[d] = y_block(col_at(d))
        ycopy(d).start()

    ysum[...] = y_block(c)

    @pl.loop(1, PEERS)
    def _(d):
        ycopy(d).wait_recv()
        ysum[...] += yrecv[d]

    yv = ysum[...]
    w = weight[...]
    z = jnp.dot(yv, w, precision=HP, preferred_element_type=F32)
    s = jax.nn.sigmoid(z)
    act_out[...] = z * s
    dz_vals = cot[...] * (s * (1.0 + z * (1.0 - s)))
    p_t = lax.dot_general(w, dz_vals, (((1,), (1,)), ((), ())), precision=HP, preferred_element_type=F32)
    pown[...] = p_t
    precv[0] = p_t

    def pcopy(d):
        return to(pown, precv.at[d], ps.at[d], pr.at[d], r, col_at(d))

    @pl.loop(1, PEERS)
    def _(d):
        pcopy(d).start()

    term = lax.dot_general(yv, dz_vals, (((0,), (0,)), ((), ())), precision=HP, preferred_element_type=F32)
    wterm[...] = term.reshape(XY, 8, B)

    def w1copy(d, owner, source):
        return to(wterm.at[lax.rem(owner, XY)], w1.at[source], w1s.at[d], w1r.at[source], r, owner)

    @pl.loop(1, PEERS)
    def _(d):
        w1copy(d, col_at(d), c).start()

    w1[c] = wterm[xy]

    for i in range(COLS):
        facc[i] = jnp.zeros((B, B), F32)

    def back(j):
        s1, s2 = col_from(2 * j), col_from(2 * j + 1)
        p = jnp.concatenate([precv[2 * j], precv[2 * j + 1]], axis=1)
        hi, lo = split(p)
        lhs = jnp.concatenate([hi, lo], axis=0)
        for i in range(COLS):
            rhs = jnp.concatenate([pieces[idx[s1 * COLS + i]], pieces[idx[s2 * COLS + i]]], axis=0)
            res = jnp.dot(lhs, rhs, preferred_element_type=F32)
            facc[i] += (res[:B, :B] + res[B:, B:]) + (res[:B, B:] + res[B:, :B])

    def back_pairs(lo, hi):
        @pl.loop(lo, hi)
        def _(j):
            pcopy(2 * j).wait_recv()
            pcopy(2 * j + 1).wait_recv()
            back(j)

    pcopy(1).wait_recv()
    back(0)
    back_pairs(1, 12)

    @pl.loop(1, PEERS)
    def _(d):
        w1copy(d, c, col_from(d)).wait_recv()

    w2[r] = jnp.sum(w1[...], axis=0)

    def w2copy(e, row, source):
        return to(w2.at[r], w2.at[source], w2s.at[e], w2r.at[source], row, c)

    @pl.loop(1, ROWS)
    def _(e):
        w2copy(e, lax.rem(r + e, ROWS), r).start()

    back_pairs(12, 14)

    @pl.loop(1, ROWS)
    def _(e):
        w2copy(e, r, lax.rem(r + ROWS - e, ROWS)).wait_recv()

    w3[xy] = jnp.sum(w2[...], axis=0)

    def w3copy(d, col, source):
        return to(w3.at[xy], w3.at[source], w3s.at[d], w3r.at[source], r, col)

    @pl.loop(1, XY)
    def _(d):
        w3copy(d, col_at(d), xy).start()

    back_pairs(14, 16)

    def scopy(q):
        return to(facc.at[q * 2 + (1 - core)], srecv.at[q], ss.at[q], sr.at[q], sib, c)

    def zcopy(d):
        return to(zsend.at[d], zrecv.at[d], zs.at[d], zr.at[d], lax.rem(zh + d, 4) * 2 + core, c)

    order = [lax.rem(zh + d, 4) for d in (1, 3, 2, 0)]
    for q in order:
        scopy(q).start()
    for d, q in zip((1, 3, 2), order):
        scopy(q).wait_recv()
        zsend[d] = facc[q * 2 + core] + srecv[q]
        zcopy(d).start()
    scopy(zh).wait_recv()
    total = facc[r] + srecv[zh]

    @pl.loop(1, XY)
    def _(d):
        w3copy(d, c, lax.rem(col_from(d), XY)).wait_recv()

    wgrad_out[...] = w3[...].reshape(B, B)

    for d in (1, 3, 2):
        zcopy(d).wait_recv()
        total = total + zrecv[d]
    fgrad_out[...] = total.T

    for dz in range(1, 4):
        xcopy(feat, r, dz, sib).wait_send()
        xcopy(feat, r, 3 + dz, sib).wait_send()
        zcopy(dz).wait_send()
    xcopy(feat, r, 0, sib).wait_send()
    for q in order:
        scopy(q).wait_send()

    @pl.loop(1, PEERS)
    def _(d):
        ycopy(d).wait_send()
        pcopy(d).wait_send()
        w1copy(d, c, c).wait_send()

    @pl.loop(1, ROWS)
    def _(e):
        w2copy(e, r, r).wait_send()

    @pl.loop(1, XY)
    def _(d):
        w3copy(d, c, xy).wait_send()


def local(features, block_values, block_rows, block_cols, live_block_count, weight, cotangent):
    slot = jnp.arange(SLOTS, dtype=jnp.int32)
    live = slot < live_block_count[0, 0]
    position = jnp.where(live, block_rows[0, 0] * COLS + block_cols[0, 0], -1)

    def last(match):
        return jnp.max(jnp.where(match, slot[None, :] + 1, 0), axis=1)

    prev = last((position[None, :] == position[:, None]) & (slot[None, :] < slot[:, None]) & live[None, :])
    idx = last(position[None, :] == jnp.arange(PEERS * COLS, dtype=jnp.int32)[:, None])
    prev = jnp.where(prev > 0, prev - 1, SLOTS)
    idx = jnp.where(idx > 0, idx - 1, SLOTS)

    vmem = pl.BlockSpec(memory_space=pltpu.VMEM)
    smem = pl.BlockSpec(memory_space=pltpu.SMEM)
    dma = pltpu.SemaphoreType.DMA
    act, wgrad, fgrad = pl.pallas_call(
        kernel,
        out_shape=[jax.ShapeDtypeStruct((B, B), F32)] * 3,
        in_specs=[smem, smem, vmem, vmem, vmem, pl.BlockSpec(memory_space=pl.ANY)],
        out_specs=[vmem, vmem, vmem],
        scratch_shapes=[
            pltpu.VMEM((SLOTS, B, B), F32),
            pltpu.VMEM((SLOTS + 1, B, B), F32),
            pltpu.VMEM((SLOTS + 1, B, 2 * B), BF16),
            pltpu.VMEM((COLS, B, B), F32),
            pltpu.VMEM((COLS, 2 * B, 2 * B), BF16),
            pltpu.VMEM((PEERS, B, B), F32),
            pltpu.VMEM((PEERS, B, B), F32),
            pltpu.VMEM((B, B), F32),
            pltpu.VMEM((B, B), F32),
            pltpu.VMEM((PEERS, B, B), F32),
            pltpu.VMEM((COLS, B, B), F32),
            pltpu.VMEM((4, B, B), F32),
            pltpu.VMEM((4, B, B), F32),
            pltpu.VMEM((4, B, B), F32),
            pltpu.VMEM((XY, 8, B), F32),
            pltpu.VMEM((PEERS, 8, B), F32),
            pltpu.VMEM((ROWS, 8, B), F32),
            pltpu.VMEM((XY, 8, B), F32),
            dma((CHUNKS,)),
            dma((7,)),
            dma((ROWS,)),
            dma((PEERS,)),
            dma((PEERS,)),
            dma((PEERS,)),
            dma((PEERS,)),
            dma((4,)),
            dma((4,)),
            dma((4,)),
            dma((4,)),
            dma((PEERS,)),
            dma((PEERS,)),
            dma((ROWS,)),
            dma((ROWS,)),
            dma((XY,)),
            dma((XY,)),
        ],
        compiler_params=pltpu.CompilerParams(
            collective_id=0, has_side_effects=True, vmem_limit_bytes=56 * 1024 * 1024
        ),
    )(prev, idx, features[0], weight, cotangent[0], block_values[0, 0])
    return act[None], wgrad, fgrad[None]


def solution(mesh):
    in_specs = (
        P("col", "row", None),
        P("row", "col", None, None, None),
        P("row", "col", None),
        P("row", "col", None),
        P("row", "col"),
        P(),
        P("row", "col", None),
    )
    out_specs = (P("row", "col", None), P(), P("col", "row", None))
    return jax.shard_map(local, mesh=mesh, in_specs=in_specs, out_specs=out_specs, check_vma=False)
```

time: 691 us -> 115 us (0.17)
  waiting for transfers between devices: 541 us -> 0 us
  Pallas kernels: 0 us -> 105 us
  matrix products: 66.5 us -> 0 us
  local copies, waits for them, and re-layouts: 44.8 us -> 4.42 us
  blocking collectives: 20.2 us -> 0 us
  between operations: 14.5 us -> 1.3 us
    psum x1 -> x0, waiting for transfers between devices: 211 us -> none  [local(): weight_grad = lax.psum(weight_term, ('row', 'col'))]
    reduce_scatter x2 -> x0, waiting for transfers between devices: 176 us -> none  [the longest x1 141 us: local(): lax.psum_scatter(jnp.einsum('bk,kif->bif', onehot, forward_prods, precisi...]
    all_gather x1 -> x0, waiting for transfers between devices: 154 us -> none  [local(): tile_grads = lax.all_gather(back_source, 'col', axis=0, tiled=True)]
    pallas_call x0 -> x1, Pallas kernels: none -> 105 us  [local(): pl.pallas_call(kernel, out_shape=[jax.ShapeDtypeStruct((B, B), F32)] * 3,...]
    dot_general x7 -> x0, matrix products: 66.5 us -> none  [the longest x1 26.2 us: local(): jnp.einsum('kij,kjf->kif', entry_values, chosen, precision=hp)]
    dot_general x4 -> x0, local copies, waits for them, and re-layouts: 26.5 us -> none  [the longest x1 11.5 us: local(): jnp.einsum('kij,kjf->kif', entry_values, chosen, precision=hp)]
    all_gather x1 -> x0, blocking collectives: 20.2 us -> none  [local(): gathered = lax.all_gather(own_feats, 'row', axis=0, tiled=True)]
    gather x2 -> x0, local copies, waits for them, and re-layouts: 16.8 us -> none  [the longest x1 11.7 us: local(): picked = jnp.take(row_blocks, brows, axis=0)]
  transfers between devices with their start and end apart: 4 -> 0, of which waited for: 4 -> 0; matrix products, arithmetic and copies ran while one was open for 8% -> 0% of each run, Pallas kernels for 0% -> 0%
where the time goes in v1:
time: 115 us; the launch traced here: 113 us
  Pallas kernels  105 us (91%)
  local copies, waits for them, and re-layouts  4.42 us (4%)
  other arithmetic  2.16 us (2%)
  between operations  1.3 us (1%)
    pallas_call x1, Pallas kernels, local(): pl.pallas_call(kernel, out_shape=[jax.ShapeDtypeStruct((B, B), F32)] * 3,...  105 us
    unnamed x3, local copies, waits for them, and re-layouts  4.42 us

profile of v1, /device:TPU:1, one launch (start us, length us, event | category | flops | bytes accessed | tf_op | source)
XLA Modules:
  0.0 113.3 jit_solution(8775618344737237480)
XLA Ops:
  1.3 0.7 multiply_add_fusion
  2.0 0.2 select_reduce_fusion.1
  2.2 0.1 select_reduce_fusion
  2.3 0.6 compare_select_fusion.idx
  2.9 0.6 compare_select_fusion.1.prev
  3.4 105.4 %shard_map.94 = (f32[128,128]{1,0:T(8,128)}, f32[128,128]{1,0:T(8,128)}, f32[128,128]{1,0:T(8,128)}) custom-call(s32[160]{0:T(256)} %compare_select_fusion.1.prev, s32[256]{0:T(256)} %compare_select_fusion.idx, f32[128,128]{1,0:T(8,128)} %bitcast.10, f32[128,128]{1,0:T(8,128)} %weight.1, f32[128,128]{1,0:T(8,128)} %bitcast.11, f32[160,128,128]{2,1,0:T(8,128)} %bitcast.9), custom_call_target="tpu_custom_call" | custom-call | tf_op jit(solution)/shard_map/pallas_call | solution.py:294
  108.9 1.5 %copy.14 = f32[1,128,128]{2,1,0:T(8,128)} copy(f32[1,128,128]{2,1,0:T(8,128)} %bitcast.13) | data formatting | bytes 131072
  110.3 1.5 %copy.15 = f32[128,128]{1,0:T(8,128)} copy(f32[128,128]{1,0:T(8,128)} %get-tuple-element.15) | data formatting | bytes 131072
  111.8 1.5 %copy.16 = f32[1,128,128]{2,1,0:T(8,128)} copy(f32[1,128,128]{2,1,0:T(8,128)} %bitcast.12) | data formatting | bytes 131072
  (2 shorter events, 0.0 us)

commit v2 on v0

v2 whole, which is shorter than its diff:
```python
import jax
import jax.numpy as jnp
from jax import lax
from jax.experimental import pallas as pl
from jax.experimental.pallas import tpu as pltpu
from jax.sharding import PartitionSpec as P

B = 128
SLOTS = 160
COLS = 8
CHUNK = 20
CHUNKS = SLOTS // CHUNK
WIDE = 256
F32 = jnp.float32
BF16 = jnp.bfloat16
HP = lax.Precision.HIGHEST


def split(v):
    hi = v.astype(BF16)
    return hi, (v - hi.astype(F32)).astype(BF16)


def kernel(
    count, rows, cols, feat, weight, cot, values,
    act_out, wgrad_out, fgrad_out,
    land, summed, pieces, posbuf, tabv, tab, xbuf, xx, cotbuf, ysend, yrecv, y2send, y2recv,
    plane, zplane, acts, pbuf, facc, srecv, zsend, zrecv,
    wterm, wa, wsum, wb, wc, wd, wz, wg,
    asem, tsem, xs, xr, cs, cr, ys, yr, y2s, y2r, es, er, ps, pr, ss, sr, zs, zr,
    was, war, wbs, wbr, wds, wdr, wzs, wzr, wys, wyr, wxs, wxr,
):
    r = lax.axis_index("row")
    c = lax.axis_index("col")
    zh, core = lax.div(r, 2), lax.rem(r, 2)
    zl, x, y = lax.div(c, 16), lax.rem(lax.div(c, 4), 4), lax.rem(c, 4)
    sib = zh * 2 + (1 - core)

    def plus(v, d):
        return lax.rem(v + d, 4)

    def col(h, at_x, at_y):
        return h * 16 + at_x * 4 + at_y

    def primary(h, a):
        return col(zl, plus(x, a * (1 - h)), plus(y, a * h))

    def second(h, q):
        return col(zl, plus(x, q * h), plus(y, q * (1 - h)))

    def to(src, dst, send, recv, row, to_col):
        return pltpu.make_async_remote_copy(
            src_ref=src, dst_ref=dst, send_sem=send, recv_sem=recv,
            device_id={"row": row, "col": to_col}, device_id_type=pl.DeviceIdType.MESH,
        )

    def loads(i):
        part = pl.ds(i * CHUNK, CHUNK)
        return pltpu.make_async_copy(values.at[part], land.at[part], asem.at[i])

    barrier = pltpu.get_barrier_semaphore()
    greeted = [(sib, c), (r, col(1 - zl, x, y))]
    for d in range(1, 4):
        greeted += [(plus(zh, d) * 2 + core, c), (r, primary(0, d)), (r, primary(1, d))]
    for row, at in greeted:
        pl.semaphore_signal(barrier, 1, device_id={"row": row, "col": at}, device_id_type=pl.DeviceIdType.MESH)

    for i in range(CHUNKS):
        loads(i).start()

    lane = lax.broadcasted_iota(jnp.int32, (1, SLOTS), 1)
    position = jnp.where(lane < count[0, 0], rows[...] * COLS + cols[...], -1)
    posbuf[...] = jnp.full((1, WIDE), -1.0, F32)
    posbuf[:, :SLOTS] = position.astype(F32)
    along = jnp.broadcast_to(posbuf[...], (WIDE, WIDE))
    down = along.T[:SLOTS]
    j = lax.broadcasted_iota(jnp.int32, (SLOTS, WIDE), 0)
    k = lax.broadcasted_iota(jnp.int32, (SLOTS, WIDE), 1)
    prev = jnp.max(jnp.where((down == along[:SLOTS]) & (j < k) & (down >= 0.0), j, -1), axis=0, keepdims=True)
    last = jnp.max(jnp.where(down == k.astype(F32), j, -1), axis=0, keepdims=True)
    tabv[0:1, :] = jnp.where(prev < 0, SLOTS, prev)
    tabv[1:2, :] = jnp.where(last < 0, SLOTS, last)
    tables = pltpu.make_async_copy(tabv, tab, tsem)
    tables.start()

    pl.semaphore_wait(barrier, len(greeted))

    def xcopy(src, slot, send, row):
        return to(src, xbuf.at[slot], xs.at[send], xr.at[slot], row, c)

    for d in (2, 1, 3):
        xcopy(feat, r, d, plus(zh, d) * 2 + core).start()
    xcopy(feat, r, 0, sib).start()
    ccopy = to(cot, cotbuf.at[zl], cs, cr, r, col(1 - zl, x, y))
    ccopy.start()
    xbuf[r] = feat[...]
    cotbuf[zl] = cot[...]

    summed[SLOTS] = jnp.zeros((B, B), F32)
    pieces[SLOTS] = jnp.zeros((B, 2 * B), BF16)
    tables.wait()

    def prepare(i):
        loads(i).wait()

        @pl.loop(i * CHUNK, (i + 1) * CHUNK)
        def _(s):
            v = land[s] + summed[tab[0, s]]
            summed[s] = v
            hi, lo = split(v)
            pieces[s, :, :B] = hi
            pieces[s, :, B:] = lo

    def block(at, i):
        return pieces[tab[1, at * COLS + i]]

    for i in range(CHUNKS):
        prepare(i)

    for d in (1, 3, 2):
        slot = plus(zh, 4 - d) * 2 + core
        xcopy(feat, slot, d, sib).wait_recv()
        xcopy(xbuf.at[slot], slot, 3 + d, sib).start()

    for d in range(4):
        slot = plus(zh, d) * 2 + (1 - core)
        xcopy(feat, slot, 0, sib).wait_recv()
    for i in range(COLS):
        hi, lo = split(xbuf[i])
        xx[i, :B, :B] = hi
        xx[i, B:, :B] = hi
        xx[i, :B, B:] = lo
        xx[i, B:, B:] = lo

    def y1copy(h, q, a):
        slot = h * 16 + q * 4 + a
        return to(ysend.at[slot], yrecv.at[slot], ys.at[slot], yr.at[slot], r, primary(h, a))

    @pl.loop(0, 8)
    def _(g):
        h, q = lax.rem(g, 2), plus(lax.div(g, 2), 1)
        at = [col(h, plus(x, a * (1 - h) + q * h), plus(y, q * (1 - h) + a * h)) for a in range(4)]
        acc = jnp.zeros((4 * B, 2 * B), F32)
        for i in range(COLS):
            lhs = jnp.concatenate([block(n, i) for n in at], axis=0)
            acc = acc + jnp.dot(lhs, xx[i], preferred_element_type=F32)
        for a in range(4):
            part = acc[a * B : (a + 1) * B]
            ysend[h * 16 + q * 4 + a] = part[:, :B] + part[:, B:]
        for a in (2, 1, 3):
            y1copy(h, q, a).start()

    def y2copy(h, q):
        slot = h * 4 + q
        return to(y2send.at[slot], y2recv.at[slot], y2s.at[slot], y2r.at[slot], r, second(h, q))

    def summed_first(h, q):
        slot = h * 16 + q * 4
        for a in range(1, 4):
            y1copy(h, q, a).wait_recv()
        return (ysend[slot] + yrecv[slot + 1]) + (yrecv[slot + 2] + yrecv[slot + 3])

    @pl.loop(0, 6)
    def _(g):
        h, q = lax.rem(g, 2), 1 + lax.div(g, 2)
        y2send[h * 4 + q] = summed_first(h, q)
        y2copy(h, q).start()

    def ecopy(h):
        return to(plane.at[h], zplane.at[h], es.at[h], er.at[h], r, col(1 - zl, x, y))

    for h in range(2):
        own = summed_first(h, 0)
        for q in range(1, 4):
            y2copy(h, q).wait_recv()
            own = own + y2recv[h * 4 + q]
        plane[h] = own
        ecopy(h).start()
    ccopy.wait_recv()
    for h in range(2):
        ecopy(h).wait_recv()

    yv = (plane[...] + zplane[...]).reshape(2 * B, B)
    w = weight[...]
    z = jnp.dot(yv, w, precision=HP, preferred_element_type=F32)
    s = jax.nn.sigmoid(z)
    dz = cotbuf[...].reshape(2 * B, B) * (s * (1.0 + z * (1.0 - s)))
    for h in range(2):
        pbuf[h * 16] = lax.dot_general(
            w, dz[h * B : (h + 1) * B], (((1,), (1,)), ((), ())), precision=HP, preferred_element_type=F32
        )

    def pcopy(h, q, a):
        slot = h * 16 + q * 4 + a
        source = slot if q == 0 or a == 0 else h * 16 + a
        where = primary(h, a) if q == 0 else second(h, q)
        if a == 0:
            source = h * 16
        elif q == 0:
            source = h * 16
        return to(pbuf.at[source], pbuf.at[slot], ps.at[slot], pr.at[slot], r, where)

    for a in (1, 3, 2):
        for h in range(2):
            pcopy(h, 0, a).start()
    for q in (1, 3, 2):
        for h in range(2):
            pcopy(h, q, 0).start()

    acts[...] = (z * s).reshape(2, B, B)
    act_out[...] = acts[zl]
    term = lax.dot_general(yv, dz, (((0,), (0,)), ((), ())), precision=HP, preferred_element_type=F32)
    wterm[...] = term.reshape(16, 8, B)

    def wacopy(a):
        there = plus(x, a)
        return to(wterm.at[pl.ds(there * 4, 4)], wa.at[a], was.at[a], war.at[a], r, primary(0, a))

    def wbcopy(a):
        return to(wsum.at[plus(y, a)], wb.at[a], wbs.at[a], wbr.at[a], r, primary(1, a))

    wdcopy = to(wc, wd, wds, wdr, sib, c)

    def wzcopy(a, slot):
        return to(wz.at[slot], wz.at[slot], wzs.at[a], wzr.at[a], plus(zh, a) * 2 + core, c)

    def wycopy(a, at_y):
        return to(wg.at[x, at_y], wg.at[x, at_y], wys.at[a], wyr.at[a], r, primary(1, a))

    def wxcopy(a, at_x):
        return to(wg.at[at_x], wg.at[at_x], wxs.at[a], wxr.at[a], r, primary(0, a))

    for a in range(1, 4):
        wacopy(a).start()
    for i in range(COLS):
        facc[i] = jnp.zeros((B, B), F32)

    for a in (1, 3, 2):
        for h in range(2):
            pcopy(h, 0, a).wait_recv()
            for q in (1, 3, 2):
                pcopy(h, q, a).start()

    def back(g):
        n = lax.div(g, 2)
        h, a = lax.rem(g, 2), lax.rem(lax.div(n * (n + 1), 2), 4)
        base = h * 16 + a
        at = []
        for q in range(4):
            at.append(col(h, plus(x + 8, -(a * (1 - h) + q * h)), plus(y + 8, -(q * (1 - h) + a * h))))
        p = jnp.concatenate([pbuf[base + q * 4] for q in range(4)], axis=1)
        hi, lo = split(p)
        lhs = jnp.concatenate([hi, lo], axis=0)
        for i in range(COLS):
            rhs = jnp.concatenate([block(m, i) for m in at], axis=0)
            res = jnp.dot(lhs, rhs, preferred_element_type=F32)
            facc[i] += (res[:B, :B] + res[B:, B:]) + (res[:B, B:] + res[B:, :B])

    def arrive(g):
        n = lax.div(g, 2)
        h, a = lax.rem(g, 2), lax.rem(lax.div(n * (n + 1), 2), 4)
        for q in range(1, 4):
            slot = h * 16 + q * 4 + a
            to(pbuf.at[slot], pbuf.at[slot], ps.at[slot], pr.at[slot], r, second(h, q)).wait_recv()

    def back_groups(lo, hi):
        @pl.loop(lo, hi)
        def _(g):
            arrive(g)
            back(g)

    back_groups(0, 2)
    for a in range(1, 4):
        wacopy(a).wait_recv()
    wsum[...] = (wterm[pl.ds(x * 4, 4)] + wa[1]) + (wa[2] + wa[3])
    for a in range(1, 4):
        wbcopy(a).start()

    back_groups(2, 4)
    for a in range(1, 4):
        wbcopy(a).wait_recv()
    wc[...] = (wsum[y] + wb[1]) + (wb[2] + wb[3])
    wdcopy.start()

    back_groups(4, 5)
    wdcopy.wait_recv()
    wz[zh] = wc[...] + wd[...]
    for a in range(1, 4):
        wzcopy(a, zh).start()

    back_groups(5, 7)
    for a in range(1, 4):
        wzcopy(a, plus(zh, 4 - a)).wait_recv()
    wg[x, y] = (wz[0] + wz[1]) + (wz[2] + wz[3])
    for a in range(1, 4):
        wycopy(a, y).start()

    back_groups(7, 8)

    def scopy(q):
        return to(facc.at[q * 2 + (1 - core)], srecv.at[q], ss.at[q], sr.at[q], sib, c)

    def zcopy(d):
        return to(zsend.at[d], zrecv.at[d], zs.at[d], zr.at[d], plus(zh, d) * 2 + core, c)

    for d in (2, 1, 3, 0):
        scopy(plus(zh, d)).start()
    for d in (2, 1, 3):
        q = plus(zh, d)
        scopy(q).wait_recv()
        zsend[d] = facc[q * 2 + core] + srecv[q]
        zcopy(d).start()
    scopy(zh).wait_recv()
    total = facc[r] + srecv[zh]

    for a in range(1, 4):
        wycopy(a, plus(y, 4 - a)).wait_recv()
    for a in range(1, 4):
        wxcopy(a, x).start()
    for a in range(1, 4):
        wxcopy(a, plus(x, 4 - a)).wait_recv()
    wgrad_out[...] = wg[...].reshape(B, B)

    ccopy.wait_send()
    wdcopy.wait_send()
    xcopy(feat, r, 0, sib).wait_send()
    for a in range(1, 4):
        xcopy(feat, r, a, sib).wait_send()
        xcopy(feat, r, 3 + a, sib).wait_send()
        wacopy(a).wait_send()
        wbcopy(a).wait_send()
        wzcopy(a, zh).wait_send()
        wycopy(a, y).wait_send()
        wxcopy(a, x).wait_send()
    for h in range(2):
        ecopy(h).wait_send()
        for q in range(4):
            scopy(q).wait_send() if h == 0 else None
            if q:
                y2copy(h, q).wait_send()
            for a in range(4):
                if a:
                    y1copy(h, q, a).wait_send()
                if a or q:
                    pcopy(h, q, a).wait_send()

    for d in (1, 3, 2):
        zcopy(d).wait_recv()
        total = total + zrecv[d]
    fgrad_out[...] = total.T
    for d in range(1, 4):
        zcopy(d).wait_send()


def deliver(a, b, c, a_out, b_out, c_out, sems):
    copies = [pltpu.make_async_copy(s, d, sems.at[i]) for i, (s, d) in enumerate([(a, a_out), (b, b_out), (c, c_out)])]
    for copy in copies:
        copy.start()
    for copy in copies:
        copy.wait()


def local(features, block_values, block_rows, block_cols, live_block_count, weight, cotangent):
    vmem = pl.BlockSpec(memory_space=pltpu.VMEM)
    smem = pl.BlockSpec(memory_space=pltpu.SMEM)
    anywhere = pl.BlockSpec(memory_space=pl.ANY)
    dma = pltpu.SemaphoreType.DMA
    results = [jax.ShapeDtypeStruct((B, B), F32)] * 3

    def blocks(n):
        return pltpu.VMEM((n, B, B), F32)

    outs = pl.pallas_call(
        kernel,
        out_shape=results,
        in_specs=[smem, vmem, vmem, vmem, vmem, vmem, anywhere],
        out_specs=[vmem, vmem, vmem],
        scratch_shapes=[
            blocks(SLOTS),
            blocks(SLOTS + 1),
            pltpu.VMEM((SLOTS + 1, B, 2 * B), BF16),
            pltpu.VMEM((1, WIDE), F32),
            pltpu.VMEM((2, WIDE), jnp.int32),
            pltpu.SMEM((2, WIDE), jnp.int32),
            blocks(COLS),
            pltpu.VMEM((COLS, 2 * B, 2 * B), BF16),
            blocks(2),
            blocks(32),
            blocks(32),
            blocks(8),
            blocks(8),
            blocks(2),
            blocks(2),
            blocks(2),
            blocks(32),
            blocks(COLS),
            blocks(4),
            blocks(4),
            blocks(4),
            pltpu.VMEM((16, 8, B), F32),
            pltpu.VMEM((4, 4, 8, B), F32),
            pltpu.VMEM((4, 8, B), F32),
            pltpu.VMEM((4, 8, B), F32),
            pltpu.VMEM((8, B), F32),
            pltpu.VMEM((8, B), F32),
            pltpu.VMEM((4, 8, B), F32),
            pltpu.VMEM((4, 4, 8, B), F32),
            dma((CHUNKS,)), dma,
            dma((7,)), dma((8,)), dma, dma,
            dma((32,)), dma((32,)), dma((8,)), dma((8,)), dma((2,)), dma((2,)),
            dma((32,)), dma((32,)), dma((4,)), dma((4,)), dma((4,)), dma((4,)),
            dma((4,)), dma((4,)), dma((4,)), dma((4,)), dma, dma,
            dma((4,)), dma((4,)), dma((4,)), dma((4,)), dma((4,)), dma((4,)),
        ],
        compiler_params=pltpu.CompilerParams(
            collective_id=0, has_side_effects=True, vmem_limit_bytes=56 * 1024 * 1024
        ),
    )(
        live_block_count, block_rows[0], block_cols[0], features[0], weight, cotangent[0], block_values[0, 0]
    )
    act, wgrad, fgrad = pl.pallas_call(
        deliver,
        out_shape=results,
        in_specs=[anywhere] * 3,
        out_specs=[anywhere] * 3,
        scratch_shapes=[dma((3,))],
    )(*outs)
    return act[None], wgrad, fgrad[None]


def solution(mesh):
    in_specs = (
        P("col", "row", None),
        P("row", "col", None, None, None),
        P("row", "col", None),
        P("row", "col", None),
        P("row", "col"),
        P(),
        P("row", "col", None),
    )
    out_specs = (P("row", "col", None), P(), P("col", "row", None))
    return jax.shard_map(local, mesh=mesh, in_specs=in_specs, out_specs=out_specs, check_vma=False)
```

time: 691 us -> 86.6 us (0.13)
  waiting for transfers between devices: 541 us -> 0 us
  Pallas kernels: 0 us -> 85.2 us
  matrix products: 66.5 us -> 0 us
  local copies, waits for them, and re-layouts: 44.8 us -> 0 us
  blocking collectives: 20.2 us -> 0 us
  between operations: 14.5 us -> 1.29 us
    psum x1 -> x0, waiting for transfers between devices: 211 us -> none  [local(): weight_grad = lax.psum(weight_term, ('row', 'col'))]
    reduce_scatter x2 -> x0, waiting for transfers between devices: 176 us -> none  [the longest x1 141 us: local(): lax.psum_scatter(jnp.einsum('bk,kif->bif', onehot, forward_prods, precisi...]
    all_gather x1 -> x0, waiting for transfers between devices: 154 us -> none  [local(): tile_grads = lax.all_gather(back_source, 'col', axis=0, tiled=True)]
    pallas_call x0 -> x2, Pallas kernels: none -> 85.2 us  [the longest x1 78.1 us: local(): pl.pallas_call(kernel, out_shape=results, in_specs=[smem, vmem, vmem, vme...]
    dot_general x7 -> x0, matrix products: 66.5 us -> none  [the longest x1 26.2 us: local(): jnp.einsum('kij,kjf->kif', entry_values, chosen, precision=hp)]
    dot_general x4 -> x0, local copies, waits for them, and re-layouts: 26.5 us -> none  [the longest x1 11.5 us: local(): jnp.einsum('kij,kjf->kif', entry_values, chosen, precision=hp)]
    all_gather x1 -> x0, blocking collectives: 20.2 us -> none  [local(): gathered = lax.all_gather(own_feats, 'row', axis=0, tiled=True)]
    gather x2 -> x0, local copies, waits for them, and re-layouts: 16.8 us -> none  [the longest x1 11.7 us: local(): picked = jnp.take(row_blocks, brows, axis=0)]
  transfers between devices with their start and end apart: 4 -> 0, of which waited for: 4 -> 0; matrix products, arithmetic and copies ran while one was open for 8% -> 0% of each run, Pallas kernels for 0% -> 0%
where the time goes in v2:
time: 86.6 us; the launch traced here: 86.4 us
  Pallas kernels  85.2 us (98%)
  between operations  1.29 us (1%)
    pallas_call x1, Pallas kernels, local(): pl.pallas_call(kernel, out_shape=results, in_specs=[smem, vmem, vmem, vme...  78.1 us
    pallas_call x1, Pallas kernels, local(): pl.pallas_call(deliver, out_shape=results, in_specs=[anywhere] * 3, out_s...  7.09 us

profile of v2, /device:TPU:1, one launch (start us, length us, event | category | flops | bytes accessed | tf_op | source)
XLA Modules:
  0.0 86.4 jit_solution(6393682259838524027)
XLA Ops:
  1.3 78.1 %shard_map.94 = (f32[128,128]{1,0:T(8,128)}, f32[128,128]{1,0:T(8,128)}, f32[128,128]{1,0:T(8,128)}) custom-call(s32[1,1]{1,0:T(1,128)S(6)} %copy.10.count, s32[1,160]{1,0:T(1,128)} %bitcast.10, s32[1,160]{1,0:T(1,128)} %bitcast.11, f32[128,128]{1,0:T(8,128)} %bitcast.8, f32[128,128]{1,0:T(8,128)} %weight.1, f32[128,128]{1,0:T(8,128)} %bitcast.9, ...), custom_call_target="tpu_custom_call" | custom-call | tf_op jit(solution)/shard_map/pallas_call | solution.py:373
  79.4 7.1 %shard_map.95 = (f32[128,128]{1,0:T(8,128)}, f32[128,128]{1,0:T(8,128)}, f32[128,128]{1,0:T(8,128)}) custom-call(f32[128,128]{1,0:T(8,128)} %get-tuple-element.9.a, f32[128,128]{1,0:T(8,128)} %get-tuple-element.10.b, f32[128,128]{1,0:T(8,128)} %get-tuple-element.11.c), custom_call_target="tpu_custom_call" | custom-call | tf_op jit(solution)/shard_map/pallas_call | solution.py:421

commit v3 on v2

--- a/solution.py
+++ b/solution.py
@@ -68,6 +68,18 @@
     for i in range(CHUNKS):
         loads(i).start()
 
+    pl.semaphore_wait(barrier, len(greeted))
+
+    def xcopy(src, slot, send, row):
+        return to(src, xbuf.at[slot], xs.at[send], xr.at[slot], row, c)
+
+    for d in (2, 1, 3):
+        xcopy(feat, r, d, plus(zh, d) * 2 + core).start()
+    xcopy(feat, r, 0, sib).start()
+    ccopy = to(cot, cotbuf.at[zl], cs, cr, r, col(1 - zl, x, y))
+    xbuf[r] = feat[...]
+    cotbuf[zl] = cot[...]
+
     lane = lax.broadcasted_iota(jnp.int32, (1, SLOTS), 1)
     position = jnp.where(lane < count[0, 0], rows[...] * COLS + cols[...], -1)
     posbuf[...] = jnp.full((1, WIDE), -1.0, F32)
@@ -83,19 +95,6 @@
     tables = pltpu.make_async_copy(tabv, tab, tsem)
     tables.start()
 
-    pl.semaphore_wait(barrier, len(greeted))
-
-    def xcopy(src, slot, send, row):
-        return to(src, xbuf.at[slot], xs.at[send], xr.at[slot], row, c)
-
-    for d in (2, 1, 3):
-        xcopy(feat, r, d, plus(zh, d) * 2 + core).start()
-    xcopy(feat, r, 0, sib).start()
-    ccopy = to(cot, cotbuf.at[zl], cs, cr, r, col(1 - zl, x, y))
-    ccopy.start()
-    xbuf[r] = feat[...]
-    cotbuf[zl] = cot[...]
-
     summed[SLOTS] = jnp.zeros((B, B), F32)
     pieces[SLOTS] = jnp.zeros((B, 2 * B), BF16)
     tables.wait()
@@ -125,6 +124,7 @@
     for d in range(4):
         slot = plus(zh, d) * 2 + (1 - core)
         xcopy(feat, slot, 0, sib).wait_recv()
+    ccopy.start()
     for i in range(COLS):
         hi, lo = split(xbuf[i])
         xx[i, :B, :B] = hi
@@ -203,35 +203,35 @@
     for a in (1, 3, 2):
         for h in range(2):
             pcopy(h, 0, a).start()
+
+    term = lax.dot_general(yv, dz, (((0,), (0,)), ((), ())), precision=HP, preferred_element_type=F32)
+    wterm[...] = term.reshape(16, 8, B)
+
+    def wacopy(a):
+        there = plus(x, a)
+        return to(wterm.at[pl.ds(there * 4, 4)], wa.at[a], was.at[a], war.at[a], r, primary(0, a))
+
+    def wbcopy(a):
+        return to(wsum.at[plus(y, a)], wb.at[a], wbs.at[a], wbr.at[a], r, primary(1, a))
+
+    wdcopy = to(wc, wd, wds, wdr, sib, c)
+
+    def wzcopy(a, slot):
+        return to(wz.at[slot], wz.at[slot], wzs.at[a], wzr.at[a], plus(zh, a) * 2 + core, c)
+
+    def wycopy(a, at_y):
+        return to(wg.at[x, at_y], wg.at[x, at_y], wys.at[a], wyr.at[a], r, primary(1, a))
+
+    def wxcopy(a, at_x):
+        return to(wg.at[at_x], wg.at[at_x], wxs.at[a], wxr.at[a], r, primary(0, a))
+
+    for a in range(1, 4):
+        wacopy(a).start()
     for q in (1, 3, 2):
         for h in range(2):
             pcopy(h, q, 0).start()
-
     acts[...] = (z * s).reshape(2, B, B)
     act_out[...] = acts[zl]
-    term = lax.dot_general(yv, dz, (((0,), (0,)), ((), ())), precision=HP, preferred_element_type=F32)
-    wterm[...] = term.reshape(16, 8, B)
-
-    def wacopy(a):
-        there = plus(x, a)
-        return to(wterm.at[pl.ds(there * 4, 4)], wa.at[a], was.at[a], war.at[a], r, primary(0, a))
-
-    def wbcopy(a):
-        return to(wsum.at[plus(y, a)], wb.at[a], wbs.at[a], wbr.at[a], r, primary(1, a))
-
-    wdcopy = to(wc, wd, wds, wdr, sib, c)
-
-    def wzcopy(a, slot):
-        return to(wz.at[slot], wz.at[slot], wzs.at[a], wzr.at[a], plus(zh, a) * 2 + core, c)
-
-    def wycopy(a, at_y):
-        return to(wg.at[x, at_y], wg.at[x, at_y], wys.at[a], wyr.at[a], r, primary(1, a))
-
-    def wxcopy(a, at_x):
-        return to(wg.at[at_x], wg.at[at_x], wxs.at[a], wxr.at[a], r, primary(0, a))
-
-    for a in range(1, 4):
-        wacopy(a).start()
     for i in range(COLS):
         facc[i] = jnp.zeros((B, B), F32)
 
@@ -240,8 +240,14 @@
             pcopy(h, 0, a).wait_recv()
             for q in (1, 3, 2):
                 pcopy(h, q, a).start()
-
-    def back(g):
+        if a == 3:
+            for d in range(1, 4):
+                wacopy(d).wait_recv()
+            wsum[...] = (wterm[pl.ds(x * 4, 4)] + wa[1]) + (wa[2] + wa[3])
+            for d in range(1, 4):
+                wbcopy(d).start()
+
+    def back(g, final=False):
         n = lax.div(g, 2)
         h, a = lax.rem(g, 2), lax.rem(lax.div(n * (n + 1), 2), 4)
         base = h * 16 + a
@@ -251,10 +257,15 @@
         p = jnp.concatenate([pbuf[base + q * 4] for q in range(4)], axis=1)
         hi, lo = split(p)
         lhs = jnp.concatenate([hi, lo], axis=0)
-        for i in range(COLS):
-            rhs = jnp.concatenate([block(m, i) for m in at], axis=0)
-            res = jnp.dot(lhs, rhs, preferred_element_type=F32)
-            facc[i] += (res[:B, :B] + res[B:, B:]) + (res[:B, B:] + res[B:, :B])
+        for d in (2, 1, 3, 0):
+            row = plus(zh, d)
+            for e in range(2):
+                i = row * 2 + e
+                rhs = jnp.concatenate([block(m, i) for m in at], axis=0)
+                res = jnp.dot(lhs, rhs, preferred_element_type=F32)
+                facc[i] += (res[:B, :B] + res[B:, B:]) + (res[:B, B:] + res[B:, :B])
+            if final:
+                scopy(row).start()
 
     def arrive(g):
         n = lax.div(g, 2)
@@ -269,14 +280,13 @@
             arrive(g)
             back(g)
 
-    back_groups(0, 2)
-    for a in range(1, 4):
-        wacopy(a).wait_recv()
-    wsum[...] = (wterm[pl.ds(x * 4, 4)] + wa[1]) + (wa[2] + wa[3])
-    for a in range(1, 4):
-        wbcopy(a).start()
-
-    back_groups(2, 4)
+    def scopy(q):
+        return to(facc.at[q * 2 + (1 - core)], srecv.at[q], ss.at[q], sr.at[q], sib, c)
+
+    def zcopy(d):
+        return to(zsend.at[d], zrecv.at[d], zs.at[d], zr.at[d], plus(zh, d) * 2 + core, c)
+
+    back_groups(0, 4)
     for a in range(1, 4):
         wbcopy(a).wait_recv()
     wc[...] = (wsum[y] + wb[1]) + (wb[2] + wb[3])
@@ -289,22 +299,9 @@
         wzcopy(a, zh).start()
 
     back_groups(5, 7)
-    for a in range(1, 4):
-        wzcopy(a, plus(zh, 4 - a)).wait_recv()
-    wg[x, y] = (wz[0] + wz[1]) + (wz[2] + wz[3])
-    for a in range(1, 4):
-        wycopy(a, y).start()
-
-    back_groups(7, 8)
-
-    def scopy(q):
-        return to(facc.at[q * 2 + (1 - core)], srecv.at[q], ss.at[q], sr.at[q], sib, c)
-
-    def zcopy(d):
-        return to(zsend.at[d], zrecv.at[d], zs.at[d], zr.at[d], plus(zh, d) * 2 + core, c)
-
-    for d in (2, 1, 3, 0):
-        scopy(plus(zh, d)).start()
+    arrive(7)
+    back(7, True)
+
     for d in (2, 1, 3):
         q = plus(zh, d)
         scopy(q).wait_recv()
@@ -312,6 +309,12 @@
         zcopy(d).start()
     scopy(zh).wait_recv()
     total = facc[r] + srecv[zh]
+
+    for a in range(1, 4):
+        wzcopy(a, plus(zh, 4 - a)).wait_recv()
+    wg[x, y] = (wz[0] + wz[1]) + (wz[2] + wz[3])
+    for a in range(1, 4):
+        wycopy(a, y).start()
 
     for a in range(1, 4):
         wycopy(a, plus(y, 4 - a)).wait_recv()
@@ -352,12 +355,10 @@
         zcopy(d).wait_send()
 
 
-def deliver(a, b, c, a_out, b_out, c_out, sems):
-    copies = [pltpu.make_async_copy(s, d, sems.at[i]) for i, (s, d) in enumerate([(a, a_out), (b, b_out), (c, c_out)])]
-    for copy in copies:
-        copy.start()
-    for copy in copies:
-        copy.wait()
+def deliver(a, b, c, a_out, b_out, c_out):
+    a_out[...] = a[...]
+    b_out[...] = b[...]
+    c_out[...] = c[...]
 
 
 def local(features, block_values, block_rows, block_cols, live_block_count, weight, cotangent):
@@ -421,9 +422,9 @@
     act, wgrad, fgrad = pl.pallas_call(
         deliver,
         out_shape=results,
-        in_specs=[anywhere] * 3,
-        out_specs=[anywhere] * 3,
-        scratch_shapes=[dma((3,))],
+        in_specs=[vmem] * 3,
+        out_specs=[vmem] * 3,
+
     )(*outs)
     return act[None], wgrad, fgrad[None]
 

time: 86.6 us -> 77.4 us (0.89)
  Pallas kernels: 85.2 us -> 76 us
    pallas_call x1, Pallas kernels: 7.09 us -> 1.58 us  [local(): pl.pallas_call(deliver, out_shape=results, in_specs=[vmem] * 3, out_specs...]
    pallas_call x1, Pallas kernels: 78.1 us -> 74.4 us  [local(): pl.pallas_call(kernel, out_shape=results, in_specs=[smem, vmem, vmem, vme...]
where the time goes in v3:
time: 77.4 us; the launch traced here: 77.3 us
  Pallas kernels  76 us (98%)
  between operations  1.29 us (2%)
    pallas_call x1, Pallas kernels, local(): pl.pallas_call(kernel, out_shape=results, in_specs=[smem, vmem, vmem, vme...  74.4 us
    pallas_call x1, Pallas kernels, local(): pl.pallas_call(deliver, out_shape=results, in_specs=[vmem] * 3, out_specs...  1.58 us

profile of v3, /device:TPU:1, one launch (start us, length us, event | category | flops | bytes accessed | tf_op | source)
XLA Modules:
  0.0 77.3 jit_solution(16843390538870335746)
XLA Ops:
  1.3 74.4 %shard_map.94 = (f32[128,128]{1,0:T(8,128)}, f32[128,128]{1,0:T(8,128)}, f32[128,128]{1,0:T(8,128)}) custom-call(s32[1,1]{1,0:T(1,128)S(6)} %copy.10.count, s32[1,160]{1,0:T(1,128)} %bitcast.10, s32[1,160]{1,0:T(1,128)} %bitcast.11, f32[128,128]{1,0:T(8,128)} %bitcast.8, f32[128,128]{1,0:T(8,128)} %weight.1, f32[128,128]{1,0:T(8,128)} %bitcast.9, ...), custom_call_target="tpu_custom_call" | custom-call | tf_op jit(solution)/shard_map/pallas_call | solution.py:374
  75.7 1.6 %shard_map.95 = (f32[128,128]{1,0:T(8,128)}, f32[128,128]{1,0:T(8,128)}, f32[128,128]{1,0:T(8,128)}) custom-call(f32[128,128]{1,0:T(8,128)} %get-tuple-element.9.a, f32[128,128]{1,0:T(8,128)} %get-tuple-element.10.b, f32[128,128]{1,0:T(8,128)} %get-tuple-element.11.c), custom_call_target="tpu_custom_call" | custom-call | tf_op jit(solution)/shard_map/pallas_call | solution.py:422

commit v4 on v3

--- a/solution.py
+++ b/solution.py
@@ -14,6 +14,9 @@
 F32 = jnp.float32
 BF16 = jnp.bfloat16
 HP = lax.Precision.HIGHEST
+
+
+H = B // 2
 
 
 def split(v):
@@ -116,96 +119,126 @@
     for i in range(CHUNKS):
         prepare(i)
 
-    for d in (1, 3, 2):
-        slot = plus(zh, 4 - d) * 2 + core
-        xcopy(feat, slot, d, sib).wait_recv()
-        xcopy(xbuf.at[slot], slot, 3 + d, sib).start()
-
-    for d in range(4):
-        slot = plus(zh, d) * 2 + (1 - core)
-        xcopy(feat, slot, 0, sib).wait_recv()
-    ccopy.start()
-    for i in range(COLS):
+    def spread(i):
         hi, lo = split(xbuf[i])
         xx[i, :B, :B] = hi
         xx[i, B:, :B] = hi
         xx[i, :B, B:] = lo
         xx[i, B:, B:] = lo
 
-    def y1copy(h, q, a):
-        slot = h * 16 + q * 4 + a
-        return to(ysend.at[slot], yrecv.at[slot], ys.at[slot], yr.at[slot], r, primary(h, a))
-
-    @pl.loop(0, 8)
-    def _(g):
-        h, q = lax.rem(g, 2), plus(lax.div(g, 2), 1)
-        at = [col(h, plus(x, a * (1 - h) + q * h), plus(y, q * (1 - h) + a * h)) for a in range(4)]
-        acc = jnp.zeros((4 * B, 2 * B), F32)
+    xcopy(feat, sib, 0, sib).wait_recv()
+    spread(r)
+    spread(sib)
+    for d in (1, 3, 2):
+        slot = plus(zh, 4 - d) * 2 + core
+        xcopy(feat, slot, d, sib).wait_recv()
+        xcopy(xbuf.at[slot], slot, 3 + d, sib).start()
+        spread(slot)
+
+    for d in (1, 3, 2):
+        slot = plus(zh, 4 - d) * 2 + (1 - core)
+        xcopy(feat, slot, 0, sib).wait_recv()
+        spread(slot)
+    ccopy.start()
+
+    def at_offset(h, dx, dy):
+        return col(h, plus(x, dx), plus(y, dy))
+
+    def half(route):
+        return pl.ds(pl.multiple_of(route * H, H), H)
+
+    def y1copy(h, route, a, p):
+        n = (h * 2 + route) * 4 + a
+        part = pl.ds(2 * p, 2)
+        sem = n * 2 + p
+        return to(ysend.at[n, part], yrecv.at[n, part], ys.at[sem], yr.at[sem], r, primary(route, a))
+
+    def unit(h, route, p):
+        at = []
+        for a in range(4):
+            for e in range(2):
+                q = plus(2 * p + e, 1)
+                at.append(at_offset(h, a * (1 - route) + q * route, q * (1 - route) + a * route))
+        acc = jnp.zeros((8 * H, 2 * B), F32)
         for i in range(COLS):
-            lhs = jnp.concatenate([block(n, i) for n in at], axis=0)
+            lhs = jnp.concatenate([pieces[tab[1, n * COLS + i], half(route)] for n in at], axis=0)
             acc = acc + jnp.dot(lhs, xx[i], preferred_element_type=F32)
         for a in range(4):
-            part = acc[a * B : (a + 1) * B]
-            ysend[h * 16 + q * 4 + a] = part[:, :B] + part[:, B:]
+            for e in range(2):
+                part = acc[(a * 2 + e) * H : (a * 2 + e + 1) * H]
+                ysend[(h * 2 + route) * 4 + a, 2 * p + e] = part[:, :B] + part[:, B:]
         for a in (2, 1, 3):
-            y1copy(h, q, a).start()
-
-    def y2copy(h, q):
-        slot = h * 4 + q
-        return to(y2send.at[slot], y2recv.at[slot], y2s.at[slot], y2r.at[slot], r, second(h, q))
-
-    def summed_first(h, q):
-        slot = h * 16 + q * 4
-        for a in range(1, 4):
-            y1copy(h, q, a).wait_recv()
-        return (ysend[slot] + yrecv[slot + 1]) + (yrecv[slot + 2] + yrecv[slot + 3])
-
-    @pl.loop(0, 6)
-    def _(g):
-        h, q = lax.rem(g, 2), 1 + lax.div(g, 2)
-        y2send[h * 4 + q] = summed_first(h, q)
-        y2copy(h, q).start()
+            y1copy(h, route, a, p).start()
+
+    def units(h, p):
+        @pl.loop(0, 2)
+        def _(route):
+            unit(h, route, p)
+
+    def y2copy(h, route, q):
+        n = (h * 2 + route) * 4 + q
+        return to(y2send.at[n], y2recv.at[n], y2s.at[n], y2r.at[n], r, second(route, q))
+
+    def y1sum(h, route, place):
+        n = (h * 2 + route) * 4
+        return (ysend[n, place] + yrecv[n + 1, place]) + (yrecv[n + 2, place] + yrecv[n + 3, place])
+
+    def relay_sums(h, p):
+        for route in range(2):
+            for a in range(1, 4):
+                y1copy(h, route, a, p).wait_recv()
+            for q in ((1, 2) if p == 0 else (3,)):
+                y2send[(h * 2 + route) * 4 + q] = y1sum(h, route, q - 1)
+                y2copy(h, route, q).start()
 
     def ecopy(h):
         return to(plane.at[h], zplane.at[h], es.at[h], er.at[h], r, col(1 - zl, x, y))
 
-    for h in range(2):
-        own = summed_first(h, 0)
-        for q in range(1, 4):
-            y2copy(h, q).wait_recv()
-            own = own + y2recv[h * 4 + q]
-        plane[h] = own
+    def exchange(h):
+        for route in range(2):
+            own = y1sum(h, route, 3)
+            for q in range(1, 4):
+                y2copy(h, route, q).wait_recv()
+                own = own + y2recv[(h * 2 + route) * 4 + q]
+            plane[h, route * H : (route + 1) * H] = own
         ecopy(h).start()
-    ccopy.wait_recv()
-    for h in range(2):
-        ecopy(h).wait_recv()
-
-    yv = (plane[...] + zplane[...]).reshape(2 * B, B)
+
     w = weight[...]
-    z = jnp.dot(yv, w, precision=HP, preferred_element_type=F32)
-    s = jax.nn.sigmoid(z)
-    dz = cotbuf[...].reshape(2 * B, B) * (s * (1.0 + z * (1.0 - s)))
-    for h in range(2):
-        pbuf[h * 16] = lax.dot_general(
-            w, dz[h * B : (h + 1) * B], (((1,), (1,)), ((), ())), precision=HP, preferred_element_type=F32
+
+    def pcopy(h, route, q, a):
+        sem = (h * 2 + route) * 16 + q * 4 + a
+        origin = 0 if q == 0 or a == 0 else a
+        dx, dy = a * (1 - route) + q * route, q * (1 - route) + a * route
+        source = h * 16 + origin * (4 - 3 * route)
+        where = primary(route, a) if q == 0 else second(route, q)
+        rows = slice(route * H, (route + 1) * H)
+        return to(
+            pbuf.at[source, rows], pbuf.at[h * 16 + dx * 4 + dy, rows], ps.at[sem], pr.at[sem], r, where
         )
 
-    def pcopy(h, q, a):
-        slot = h * 16 + q * 4 + a
-        source = slot if q == 0 or a == 0 else h * 16 + a
-        where = primary(h, a) if q == 0 else second(h, q)
-        if a == 0:
-            source = h * 16
-        elif q == 0:
-            source = h * 16
-        return to(pbuf.at[source], pbuf.at[slot], ps.at[slot], pr.at[slot], r, where)
-
-    for a in (1, 3, 2):
-        for h in range(2):
-            pcopy(h, 0, a).start()
-
-    term = lax.dot_general(yv, dz, (((0,), (0,)), ((), ())), precision=HP, preferred_element_type=F32)
-    wterm[...] = term.reshape(16, 8, B)
+    def middle(h):
+        yv = plane[h] + zplane[h]
+        z = jnp.dot(yv, w, precision=HP, preferred_element_type=F32)
+        s = jax.nn.sigmoid(z)
+        dz = cotbuf[h] * (s * (1.0 + z * (1.0 - s)))
+        pbuf[h * 16] = lax.dot_general(w, dz, (((1,), (1,)), ((), ())), precision=HP, preferred_element_type=F32)
+        for a in (1, 3, 2):
+            for route in range(2):
+                pcopy(h, route, 0, a).start()
+        term = lax.dot_general(yv, dz, (((0,), (0,)), ((), ())), precision=HP, preferred_element_type=F32)
+        acts[h] = z * s
+        return term.reshape(16, 8, B)
+
+    def direct(h):
+        for q in (1, 3, 2):
+            for route in range(2):
+                pcopy(h, route, q, 0).start()
+
+    def relay(h, a):
+        for route in range(2):
+            pcopy(h, route, 0, a).wait_recv()
+            for q in (1, 3, 2):
+                pcopy(h, route, q, a).start()
 
     def wacopy(a):
         there = plus(x, a)
@@ -225,37 +258,19 @@
     def wxcopy(a, at_x):
         return to(wg.at[at_x], wg.at[at_x], wxs.at[a], wxr.at[a], r, primary(0, a))
 
-    for a in range(1, 4):
-        wacopy(a).start()
-    for q in (1, 3, 2):
-        for h in range(2):
-            pcopy(h, q, 0).start()
-    acts[...] = (z * s).reshape(2, B, B)
-    act_out[...] = acts[zl]
-    for i in range(COLS):
-        facc[i] = jnp.zeros((B, B), F32)
-
-    for a in (1, 3, 2):
-        for h in range(2):
-            pcopy(h, 0, a).wait_recv()
-            for q in (1, 3, 2):
-                pcopy(h, q, a).start()
-        if a == 3:
-            for d in range(1, 4):
-                wacopy(d).wait_recv()
-            wsum[...] = (wterm[pl.ds(x * 4, 4)] + wa[1]) + (wa[2] + wa[3])
-            for d in range(1, 4):
-                wbcopy(d).start()
-
-    def back(g, final=False):
-        n = lax.div(g, 2)
-        h, a = lax.rem(g, 2), lax.rem(lax.div(n * (n + 1), 2), 4)
-        base = h * 16 + a
-        at = []
+    def scopy(q):
+        return to(facc.at[q * 2 + (1 - core)], srecv.at[q], ss.at[q], sr.at[q], sib, c)
+
+    def zcopy(d):
+        return to(zsend.at[d], zrecv.at[d], zs.at[d], zr.at[d], plus(zh, d) * 2 + core, c)
+
+    def back(h, route, a, final=False):
+        at, ps_t = [], []
         for q in range(4):
-            at.append(col(h, plus(x + 8, -(a * (1 - h) + q * h)), plus(y + 8, -(q * (1 - h) + a * h))))
-        p = jnp.concatenate([pbuf[base + q * 4] for q in range(4)], axis=1)
-        hi, lo = split(p)
+            dx, dy = a * (1 - route) + q * route, q * (1 - route) + a * route
+            at.append(col(h, plus(x + 4, -dx), plus(y + 4, -dy)))
+            ps_t.append(pbuf[h * 16 + dx * 4 + dy, half(route)])
+        hi, lo = split(jnp.concatenate(ps_t, axis=1))
         lhs = jnp.concatenate([hi, lo], axis=0)
         for d in (2, 1, 3, 0):
             row = plus(zh, d)
@@ -263,44 +278,72 @@
                 i = row * 2 + e
                 rhs = jnp.concatenate([block(m, i) for m in at], axis=0)
                 res = jnp.dot(lhs, rhs, preferred_element_type=F32)
-                facc[i] += (res[:B, :B] + res[B:, B:]) + (res[:B, B:] + res[B:, :B])
+                facc[i, half(route)] += (res[:H, :B] + res[H:, B:]) + (res[:H, B:] + res[H:, :B])
             if final:
                 scopy(row).start()
 
-    def arrive(g):
-        n = lax.div(g, 2)
-        h, a = lax.rem(g, 2), lax.rem(lax.div(n * (n + 1), 2), 4)
+    def arrive(h, route, a):
+        dy = a * route
         for q in range(1, 4):
-            slot = h * 16 + q * 4 + a
-            to(pbuf.at[slot], pbuf.at[slot], ps.at[slot], pr.at[slot], r, second(h, q)).wait_recv()
-
-    def back_groups(lo, hi):
+            sem = (h * 2 + route) * 16 + q * 4 + a
+            place = pbuf.at[h * 16 + (a * (1 - route) + q * route) * 4 + q * (1 - route) + dy, half(route)]
+            to(place, place, ps.at[sem], pr.at[sem], r, second(route, q)).wait_recv()
+
+    def back_groups(h, lo, hi):
         @pl.loop(lo, hi)
         def _(g):
-            arrive(g)
-            back(g)
-
-    def scopy(q):
-        return to(facc.at[q * 2 + (1 - core)], srecv.at[q], ss.at[q], sr.at[q], sib, c)
-
-    def zcopy(d):
-        return to(zsend.at[d], zrecv.at[d], zs.at[d], zr.at[d], plus(zh, d) * 2 + core, c)
-
-    back_groups(0, 4)
+            n = lax.div(g, 2)
+            route, a = lax.rem(g, 2), lax.rem(lax.div(n * (n + 1), 2), 4)
+            arrive(h, route, a)
+            back(h, route, a)
+
+    units(0, 0)
+    units(0, 1)
+    units(1, 0)
+    relay_sums(0, 0)
+    relay_sums(0, 1)
+    units(1, 1)
+    relay_sums(1, 0)
+    exchange(0)
+    for i in range(COLS):
+        facc[i] = jnp.zeros((B, B), F32)
+    relay_sums(1, 1)
+    ccopy.wait_recv()
+    ecopy(0).wait_recv()
+    wterm[...] = middle(0)
+    direct(0)
+    exchange(1)
+    for a in (1, 3, 2):
+        relay(0, a)
+    ecopy(1).wait_recv()
+    wterm[...] += middle(1)
+    for a in range(1, 4):
+        wacopy(a).start()
+    direct(1)
+    act_out[...] = acts[zl]
+
+    back_groups(0, 0, 6)
+    for a in range(1, 4):
+        wacopy(a).wait_recv()
+    wsum[...] = (wterm[pl.ds(x * 4, 4)] + wa[1]) + (wa[2] + wa[3])
+    for a in range(1, 4):
+        wbcopy(a).start()
+    for a in (1, 3, 2):
+        relay(1, a)
+    back_groups(0, 6, 8)
+    back_groups(1, 0, 2)
     for a in range(1, 4):
         wbcopy(a).wait_recv()
     wc[...] = (wsum[y] + wb[1]) + (wb[2] + wb[3])
     wdcopy.start()
-
-    back_groups(4, 5)
+    back_groups(1, 2, 4)
     wdcopy.wait_recv()
     wz[zh] = wc[...] + wd[...]
     for a in range(1, 4):
         wzcopy(a, zh).start()
-
-    back_groups(5, 7)
-    arrive(7)
-    back(7, True)
+    back_groups(1, 4, 7)
+    arrive(1, 1, 2)
+    back(1, 1, 2, True)
 
     for d in (2, 1, 3):
         q = plus(zh, d)
@@ -335,17 +378,19 @@
         wzcopy(a, zh).wait_send()
         wycopy(a, y).wait_send()
         wxcopy(a, x).wait_send()
+    for q in range(4):
+        scopy(q).wait_send()
     for h in range(2):
         ecopy(h).wait_send()
-        for q in range(4):
-            scopy(q).wait_send() if h == 0 else None
-            if q:
-                y2copy(h, q).wait_send()
-            for a in range(4):
-                if a:
-                    y1copy(h, q, a).wait_send()
-                if a or q:
-                    pcopy(h, q, a).wait_send()
+        for route in range(2):
+            for a in range(1, 4):
+                y1copy(h, route, a, 0).wait_send()
+                y1copy(h, route, a, 1).wait_send()
+                y2copy(h, route, a).wait_send()
+            for q in range(4):
+                for a in range(4):
+                    if a or q:
+                        pcopy(h, route, q, a).wait_send()
 
     for d in (1, 3, 2):
         zcopy(d).wait_recv()
@@ -386,10 +431,10 @@
             blocks(COLS),
             pltpu.VMEM((COLS, 2 * B, 2 * B), BF16),
             blocks(2),
-            blocks(32),
-            blocks(32),
-            blocks(8),
-            blocks(8),
+            pltpu.VMEM((16, 4, H, B), F32),
+            pltpu.VMEM((16, 4, H, B), F32),
+            pltpu.VMEM((16, H, B), F32),
+            pltpu.VMEM((16, H, B), F32),
             blocks(2),
             blocks(2),
             blocks(2),
@@ -408,8 +453,8 @@
             pltpu.VMEM((4, 4, 8, B), F32),
             dma((CHUNKS,)), dma,
             dma((7,)), dma((8,)), dma, dma,
-            dma((32,)), dma((32,)), dma((8,)), dma((8,)), dma((2,)), dma((2,)),
-            dma((32,)), dma((32,)), dma((4,)), dma((4,)), dma((4,)), dma((4,)),
+            dma((32,)), dma((32,)), dma((16,)), dma((16,)), dma((2,)), dma((2,)),
+            dma((64,)), dma((64,)), dma((4,)), dma((4,)), dma((4,)), dma((4,)),
             dma((4,)), dma((4,)), dma((4,)), dma((4,)), dma, dma,
             dma((4,)), dma((4,)), dma((4,)), dma((4,)), dma((4,)), dma((4,)),
         ],

time: 77.4 us -> 74.9 us (0.968)
  Pallas kernels: 76 us -> 73.4 us
    pallas_call x1, Pallas kernels: 74.4 us -> 71.8 us  [local(): pl.pallas_call(kernel, out_shape=results, in_specs=[smem, vmem, vmem, vme...]
where the time goes in v4:
time: 74.9 us; the launch traced here: 74.7 us
  Pallas kernels  73.4 us (98%)
  between operations  1.29 us (2%)
    pallas_call x1, Pallas kernels, local(): pl.pallas_call(kernel, out_shape=results, in_specs=[smem, vmem, vmem, vme...  71.8 us
    pallas_call x1, Pallas kernels, local(): pl.pallas_call(deliver, out_shape=results, in_specs=[vmem] * 3, out_specs...  1.58 us

profile of v4, /device:TPU:1, one launch (start us, length us, event | category | flops | bytes accessed | tf_op | source)
XLA Modules:
  0.0 74.7 jit_solution(17915604244708454267)
XLA Ops:
  1.3 71.8 %shard_map.94 = (f32[128,128]{1,0:T(8,128)}, f32[128,128]{1,0:T(8,128)}, f32[128,128]{1,0:T(8,128)}) custom-call(s32[1,1]{1,0:T(1,128)S(6)} %copy.10.count, s32[1,160]{1,0:T(1,128)} %bitcast.10, s32[1,160]{1,0:T(1,128)} %bitcast.11, f32[128,128]{1,0:T(8,128)} %bitcast.8, f32[128,128]{1,0:T(8,128)} %weight.1, f32[128,128]{1,0:T(8,128)} %bitcast.9, ...), custom_call_target="tpu_custom_call" | custom-call | tf_op jit(solution)/shard_map/pallas_call | solution.py:419
  73.1 1.6 %shard_map.95 = (f32[128,128]{1,0:T(8,128)}, f32[128,128]{1,0:T(8,128)}, f32[128,128]{1,0:T(8,128)}) custom-call(f32[128,128]{1,0:T(8,128)} %get-tuple-element.9.a, f32[128,128]{1,0:T(8,128)} %get-tuple-element.10.b, f32[128,128]{1,0:T(8,128)} %get-tuple-element.11.c), custom_call_target="tpu_custom_call" | custom-call | tf_op jit(solution)/shard_map/pallas_call | solution.py:467

commit v5 on v4

--- a/solution.py
+++ b/solution.py
@@ -25,12 +25,12 @@
 
 
 def kernel(
-    count, rows, cols, feat, weight, cot, values,
+    count, rows_in, cols_in, feat, weight_in, cot, values,
     act_out, wgrad_out, fgrad_out,
-    land, summed, pieces, posbuf, tabv, tab, xbuf, xx, cotbuf, ysend, yrecv, y2send, y2recv,
+    rows, cols, weight, land, summed, pieces, posbuf, tabv, tab, xbuf, xx, cotbuf, ysend, yrecv, y2send, y2recv,
     plane, zplane, acts, pbuf, facc, srecv, zsend, zrecv,
     wterm, wa, wsum, wb, wc, wd, wz, wg,
-    asem, tsem, xs, xr, cs, cr, ys, yr, y2s, y2r, es, er, ps, pr, ss, sr, zs, zr,
+    isem, asem, tsem, xs, xr, cs, cr, ys, yr, y2s, y2r, es, er, ps, pr, ss, sr, zs, zr,
     was, war, wbs, wbr, wds, wdr, wzs, wzr, wys, wyr, wxs, wxr,
 ):
     r = lax.axis_index("row")
@@ -68,6 +68,10 @@
     for row, at in greeted:
         pl.semaphore_signal(barrier, 1, device_id={"row": row, "col": at}, device_id_type=pl.DeviceIdType.MESH)
 
+    inputs = [(feat, xbuf.at[r]), (rows_in, rows), (cols_in, cols), (cot, cotbuf.at[zl]), (weight_in.at[0], weight)]
+    fetch = [pltpu.make_async_copy(src, dst, isem.at[i]) for i, (src, dst) in enumerate(inputs)]
+    for copy in fetch:
+        copy.start()
     for i in range(CHUNKS):
         loads(i).start()
 
@@ -76,13 +80,14 @@
     def xcopy(src, slot, send, row):
         return to(src, xbuf.at[slot], xs.at[send], xr.at[slot], row, c)
 
+    fetch[0].wait()
     for d in (2, 1, 3):
-        xcopy(feat, r, d, plus(zh, d) * 2 + core).start()
-    xcopy(feat, r, 0, sib).start()
-    ccopy = to(cot, cotbuf.at[zl], cs, cr, r, col(1 - zl, x, y))
-    xbuf[r] = feat[...]
-    cotbuf[zl] = cot[...]
-
+        xcopy(xbuf.at[r], r, d, plus(zh, d) * 2 + core).start()
+    xcopy(xbuf.at[r], r, 0, sib).start()
+    ccopy = to(cotbuf.at[zl], cotbuf.at[zl], cs, cr, r, col(1 - zl, x, y))
+
+    for copy in fetch[1:]:
+        copy.wait()
     lane = lax.broadcasted_iota(jnp.int32, (1, SLOTS), 1)
     position = jnp.where(lane < count[0, 0], rows[...] * COLS + cols[...], -1)
     posbuf[...] = jnp.full((1, WIDE), -1.0, F32)
@@ -126,18 +131,18 @@
         xx[i, :B, B:] = lo
         xx[i, B:, B:] = lo
 
-    xcopy(feat, sib, 0, sib).wait_recv()
+    xcopy(xbuf.at[r], sib, 0, sib).wait_recv()
     spread(r)
     spread(sib)
     for d in (1, 3, 2):
         slot = plus(zh, 4 - d) * 2 + core
-        xcopy(feat, slot, d, sib).wait_recv()
+        xcopy(xbuf.at[r], slot, d, sib).wait_recv()
         xcopy(xbuf.at[slot], slot, 3 + d, sib).start()
         spread(slot)
 
     for d in (1, 3, 2):
         slot = plus(zh, 4 - d) * 2 + (1 - core)
-        xcopy(feat, slot, 0, sib).wait_recv()
+        xcopy(xbuf.at[r], slot, 0, sib).wait_recv()
         spread(slot)
     ccopy.start()
 
@@ -191,8 +196,10 @@
                 y2send[(h * 2 + route) * 4 + q] = y1sum(h, route, q - 1)
                 y2copy(h, route, q).start()
 
-    def ecopy(h):
-        return to(plane.at[h], zplane.at[h], es.at[h], er.at[h], r, col(1 - zl, x, y))
+    def ecopy(h, route):
+        rows = slice(route * H, (route + 1) * H)
+        n = h * 2 + route
+        return to(plane.at[h, rows], zplane.at[h, rows], es.at[n], er.at[n], r, col(1 - zl, x, y))
 
     def exchange(h):
         for route in range(2):
@@ -201,7 +208,7 @@
                 y2copy(h, route, q).wait_recv()
                 own = own + y2recv[(h * 2 + route) * 4 + q]
             plane[h, route * H : (route + 1) * H] = own
-        ecopy(h).start()
+            ecopy(h, route).start()
 
     w = weight[...]
 
@@ -309,25 +316,28 @@
         facc[i] = jnp.zeros((B, B), F32)
     relay_sums(1, 1)
     ccopy.wait_recv()
-    ecopy(0).wait_recv()
+    ecopy(0, 0).wait_recv()
+    ecopy(0, 1).wait_recv()
     wterm[...] = middle(0)
     direct(0)
     exchange(1)
     for a in (1, 3, 2):
         relay(0, a)
-    ecopy(1).wait_recv()
+    ecopy(1, 0).wait_recv()
+    ecopy(1, 1).wait_recv()
     wterm[...] += middle(1)
     for a in range(1, 4):
         wacopy(a).start()
     direct(1)
     act_out[...] = acts[zl]
 
-    back_groups(0, 0, 6)
+    back_groups(0, 0, 4)
     for a in range(1, 4):
         wacopy(a).wait_recv()
     wsum[...] = (wterm[pl.ds(x * 4, 4)] + wa[1]) + (wa[2] + wa[3])
     for a in range(1, 4):
         wbcopy(a).start()
+    back_groups(0, 4, 6)
     for a in (1, 3, 2):
         relay(1, a)
     back_groups(0, 6, 8)
@@ -369,10 +379,10 @@
 
     ccopy.wait_send()
     wdcopy.wait_send()
-    xcopy(feat, r, 0, sib).wait_send()
-    for a in range(1, 4):
-        xcopy(feat, r, a, sib).wait_send()
-        xcopy(feat, r, 3 + a, sib).wait_send()
+    xcopy(xbuf.at[r], r, 0, sib).wait_send()
+    for a in range(1, 4):
+        xcopy(xbuf.at[r], r, a, sib).wait_send()
+        xcopy(xbuf.at[r], r, 3 + a, sib).wait_send()
         wacopy(a).wait_send()
         wbcopy(a).wait_send()
         wzcopy(a, zh).wait_send()
@@ -381,8 +391,8 @@
     for q in range(4):
         scopy(q).wait_send()
     for h in range(2):
-        ecopy(h).wait_send()
         for route in range(2):
+            ecopy(h, route).wait_send()
             for a in range(1, 4):
                 y1copy(h, route, a, 0).wait_send()
                 y1copy(h, route, a, 1).wait_send()
@@ -408,7 +418,6 @@
 
 def local(features, block_values, block_rows, block_cols, live_block_count, weight, cotangent):
     vmem = pl.BlockSpec(memory_space=pltpu.VMEM)
-    smem = pl.BlockSpec(memory_space=pltpu.SMEM)
     anywhere = pl.BlockSpec(memory_space=pl.ANY)
     dma = pltpu.SemaphoreType.DMA
     results = [jax.ShapeDtypeStruct((B, B), F32)] * 3
@@ -419,9 +428,12 @@
     outs = pl.pallas_call(
         kernel,
         out_shape=results,
-        in_specs=[smem, vmem, vmem, vmem, vmem, vmem, anywhere],
+        in_specs=[pl.BlockSpec(memory_space=pltpu.SMEM)] + [anywhere] * 6,
         out_specs=[vmem, vmem, vmem],
         scratch_shapes=[
+            pltpu.VMEM((1, SLOTS), jnp.int32),
+            pltpu.VMEM((1, SLOTS), jnp.int32),
+            pltpu.VMEM((B, B), F32),
             blocks(SLOTS),
             blocks(SLOTS + 1),
             pltpu.VMEM((SLOTS + 1, B, 2 * B), BF16),
@@ -451,9 +463,9 @@
             pltpu.VMEM((8, B), F32),
             pltpu.VMEM((4, 8, B), F32),
             pltpu.VMEM((4, 4, 8, B), F32),
-            dma((CHUNKS,)), dma,
+            dma((5,)), dma((CHUNKS,)), dma,
             dma((7,)), dma((8,)), dma, dma,
-            dma((32,)), dma((32,)), dma((16,)), dma((16,)), dma((2,)), dma((2,)),
+            dma((32,)), dma((32,)), dma((16,)), dma((16,)), dma((4,)), dma((4,)),
             dma((64,)), dma((64,)), dma((4,)), dma((4,)), dma((4,)), dma((4,)),
             dma((4,)), dma((4,)), dma((4,)), dma((4,)), dma, dma,
             dma((4,)), dma((4,)), dma((4,)), dma((4,)), dma((4,)), dma((4,)),
@@ -462,7 +474,7 @@
             collective_id=0, has_side_effects=True, vmem_limit_bytes=56 * 1024 * 1024
         ),
     )(
-        live_block_count, block_rows[0], block_cols[0], features[0], weight, cotangent[0], block_values[0, 0]
+        live_block_count, block_rows[0], block_cols[0], features[0], weight[None], cotangent[0], block_values[0, 0]
     )
     act, wgrad, fgrad = pl.pallas_call(
         deliver,

time: 74.9 us -> 73.6 us (0.983)
  Pallas kernels: 73.4 us -> 72.2 us
    pallas_call x1, Pallas kernels: 71.8 us -> 70.6 us  [local(): pl.pallas_call(kernel, out_shape=results, in_specs=[pl.BlockSpec(memory_s...]
where the time goes in v5:
time: 73.6 us; the launch traced here: 73.5 us
  Pallas kernels  72.2 us (98%)
  between operations  1.29 us (2%)
    pallas_call x1, Pallas kernels, local(): pl.pallas_call(kernel, out_shape=results, in_specs=[pl.BlockSpec(memory_s...  70.6 us
    pallas_call x1, Pallas kernels, local(): pl.pallas_call(deliver, out_shape=results, in_specs=[vmem] * 3, out_specs...  1.58 us

profile of v5, /device:TPU:1, one launch (start us, length us, event | category | flops | bytes accessed | tf_op | source)
XLA Modules:
  0.0 73.5 jit_solution(6156260786375222027)
XLA Ops:
  1.3 70.6 %shard_map.94 = (f32[128,128]{1,0:T(8,128)}, f32[128,128]{1,0:T(8,128)}, f32[128,128]{1,0:T(8,128)}) custom-call(s32[1,1]{1,0:T(1,128)S(6)} %copy.10.count, s32[1,160]{1,0:T(1,128)} %bitcast.12, s32[1,160]{1,0:T(1,128)} %bitcast.13, f32[128,128]{1,0:T(8,128)} %bitcast.9, f32[1,128,128]{2,1,0:T(8,128)} %bitcast.10, f32[128,128]{1,0:T(8,128)} %bitcast.11, ...), custom_call_target="tpu_custom_call" | custom-call | tf_op jit(solution)/shard_map/pallas_call | solution.py:428
  71.9 1.6 %shard_map.95 = (f32[128,128]{1,0:T(8,128)}, f32[128,128]{1,0:T(8,128)}, f32[128,128]{1,0:T(8,128)}) custom-call(f32[128,128]{1,0:T(8,128)} %get-tuple-element.9.a, f32[128,128]{1,0:T(8,128)} %get-tuple-element.10.b, f32[128,128]{1,0:T(8,128)} %get-tuple-element.11.c), custom_call_target="tpu_custom_call" | custom-call | tf_op jit(solution)/shard_map/pallas_call | solution.py:479

commit v6 on v5

--- a/solution.py
+++ b/solution.py
@@ -331,14 +331,14 @@
     direct(1)
     act_out[...] = acts[zl]
 
-    back_groups(0, 0, 4)
+    back_groups(0, 0, 6)
+    relay(1, 1)
     for a in range(1, 4):
         wacopy(a).wait_recv()
     wsum[...] = (wterm[pl.ds(x * 4, 4)] + wa[1]) + (wa[2] + wa[3])
     for a in range(1, 4):
         wbcopy(a).start()
-    back_groups(0, 4, 6)
-    for a in (1, 3, 2):
+    for a in (3, 2):
         relay(1, a)
     back_groups(0, 6, 8)
     back_groups(1, 0, 2)

time: 73.6 us -> 72.4 us (0.984)
  Pallas kernels: 72.2 us -> 70.8 us
    pallas_call x1, Pallas kernels: 70.6 us -> 69.3 us  [local(): pl.pallas_call(kernel, out_shape=results, in_specs=[pl.BlockSpec(memory_s...]
where the time goes in v6:
time: 72.4 us; the launch traced here: 72.1 us
  Pallas kernels  70.8 us (98%)
  between operations  1.29 us (2%)
    pallas_call x1, Pallas kernels, local(): pl.pallas_call(kernel, out_shape=results, in_specs=[pl.BlockSpec(memory_s...  69.3 us
    pallas_call x1, Pallas kernels, local(): pl.pallas_call(deliver, out_shape=results, in_specs=[vmem] * 3, out_specs...  1.58 us

profile of v6, /device:TPU:1, one launch (start us, length us, event | category | flops | bytes accessed | tf_op | source)
XLA Modules:
  0.0 72.1 jit_solution(5407560771671510684)
XLA Ops:
  1.3 69.3 %shard_map.94 = (f32[128,128]{1,0:T(8,128)}, f32[128,128]{1,0:T(8,128)}, f32[128,128]{1,0:T(8,128)}) custom-call(s32[1,1]{1,0:T(1,128)S(6)} %copy.10.count, s32[1,160]{1,0:T(1,128)} %bitcast.12, s32[1,160]{1,0:T(1,128)} %bitcast.13, f32[128,128]{1,0:T(8,128)} %bitcast.9, f32[1,128,128]{2,1,0:T(8,128)} %bitcast.10, f32[128,128]{1,0:T(8,128)} %bitcast.11, ...), custom_call_target="tpu_custom_call" | custom-call | tf_op jit(solution)/shard_map/pallas_call | solution.py:428
  70.5 1.6 %shard_map.95 = (f32[128,128]{1,0:T(8,128)}, f32[128,128]{1,0:T(8,128)}, f32[128,128]{1,0:T(8,128)}) custom-call(f32[128,128]{1,0:T(8,128)} %get-tuple-element.9.a, f32[128,128]{1,0:T(8,128)} %get-tuple-element.10.b, f32[128,128]{1,0:T(8,128)} %get-tuple-element.11.c), custom_call_target="tpu_custom_call" | custom-call | tf_op jit(solution)/shard_map/pallas_call | solution.py:479

commit v7 on v6

--- a/solution.py
+++ b/solution.py
@@ -338,9 +338,10 @@
     wsum[...] = (wterm[pl.ds(x * 4, 4)] + wa[1]) + (wa[2] + wa[3])
     for a in range(1, 4):
         wbcopy(a).start()
-    for a in (3, 2):
-        relay(1, a)
-    back_groups(0, 6, 8)
+    relay(1, 3)
+    back_groups(0, 6, 7)
+    relay(1, 2)
+    back_groups(0, 7, 8)
     back_groups(1, 0, 2)
     for a in range(1, 4):
         wbcopy(a).wait_recv()

time: 72.4 us -> 73.2 us (1.011)
  Pallas kernels: 70.8 us -> 71.8 us
    pallas_call x1, Pallas kernels: 69.3 us -> 70.2 us  [local(): pl.pallas_call(kernel, out_shape=results, in_specs=[pl.BlockSpec(memory_s...]
where the time goes in v7:
time: 73.2 us; the launch traced here: 73 us
  Pallas kernels  71.8 us (98%)
  between operations  1.29 us (2%)
    pallas_call x1, Pallas kernels, local(): pl.pallas_call(kernel, out_shape=results, in_specs=[pl.BlockSpec(memory_s...  70.2 us
    pallas_call x1, Pallas kernels, local(): pl.pallas_call(deliver, out_shape=results, in_specs=[vmem] * 3, out_specs...  1.58 us

profile of v7, /device:TPU:1, one launch (start us, length us, event | category | flops | bytes accessed | tf_op | source)
XLA Modules:
  0.0 73.0 jit_solution(11011123260669179354)
XLA Ops:
  1.3 70.2 %shard_map.94 = (f32[128,128]{1,0:T(8,128)}, f32[128,128]{1,0:T(8,128)}, f32[128,128]{1,0:T(8,128)}) custom-call(s32[1,1]{1,0:T(1,128)S(6)} %copy.10.count, s32[1,160]{1,0:T(1,128)} %bitcast.12, s32[1,160]{1,0:T(1,128)} %bitcast.13, f32[128,128]{1,0:T(8,128)} %bitcast.9, f32[1,128,128]{2,1,0:T(8,128)} %bitcast.10, f32[128,128]{1,0:T(8,128)} %bitcast.11, ...), custom_call_target="tpu_custom_call" | custom-call | tf_op jit(solution)/shard_map/pallas_call | solution.py:429
  71.5 1.6 %shard_map.95 = (f32[128,128]{1,0:T(8,128)}, f32[128,128]{1,0:T(8,128)}, f32[128,128]{1,0:T(8,128)}) custom-call(f32[128,128]{1,0:T(8,128)} %get-tuple-element.9.a, f32[128,128]{1,0:T(8,128)} %get-tuple-element.10.b, f32[128,128]{1,0:T(8,128)} %get-tuple-element.11.c), custom_call_target="tpu_custom_call" | custom-call | tf_op jit(solution)/shard_map/pallas_call | solution.py:480
